TPU v7x, 512 devices: a whole 4x4x16 slice. The times are simulated.
512 devices in a mesh: dp: 32 (over x_lo, z), head: 16 (over y, x_hi, core).
Axes of the slice: x: 4 (x_hi: 2, x_lo: 2; x = x_hi * 2 + x_lo), y: 4, z: 16, core: 2. Of those that a mesh axis runs over, the one named last changes fastest.
Arguments:
- q_latent: bfloat16 [24576, 1536], P('dp'), may hold values from -65 to 65
- kv_latent: bfloat16 [24576, 512], P('dp'), may hold values from -65 to 65
- q_cotangent: bfloat16 [24576, 6144], P('dp', 'head'), may hold values from -36 to 36
- kv_cotangent: bfloat16 [24576, 8192], P('dp', 'head'), may hold values from -36 to 36
Outputs:
- q_update: float32 [1536, 6144], P('dp', 'head')
- kv_update: float32 [512, 8192], P('dp', 'head')
All inputs are finite; a program needn't handle non-finite values.
Results may differ from a plain program's by a relative error of at most 0.0004.
Values sent between devices are 32-bit elements; how exact they have to be, the bound alone decides.
No kernel may reach another device: no remote copies, remote signals or barrier semaphores. Data moves between devices by JAX's collectives and lax.ppermute only.
A program may use at most 64 MiB of HBM per device.

v0:
```python
import math

import jax
import jax.numpy as jnp
from jax import lax
from jax.sharding import PartitionSpec as P

QRANK = 1536
KVRANK = 512
QDIM = 192
KVDIM = 256
ITERS = 5


COEF_A = 3.4445
COEF_B = -4.775
COEF_C = 2.0315
EPSILON = 1e-06


def latent_term(latent, cotangent):
    return lax.dot_general(
        latent, cotangent, (((0,), (0,)), ((), ())), preferred_element_type=jnp.float32
    )


def newton_schulz(blocks, norm_sum, gram_sum):
    squares = tuple((jnp.sum(matrix * matrix, axis=(0, 2)) for matrix in blocks))
    totals = norm_sum(squares)
    current = tuple(
        (
            matrix * lax.rsqrt(summed + EPSILON)[None, :, None]
            for matrix, summed in zip(blocks, totals)
        )
    )
    for sweep_idx in range(ITERS):
        local_grams = tuple(
            (
                jnp.einsum("rhi,rhj->hij", matrix, matrix, precision=lax.Precision.HIGHEST)
                for matrix in current
            )
        )
        gram_set = gram_sum(local_grams)
        updated = []
        for matrix, gram_mat in zip(current, gram_set):
            square_mat = jnp.einsum(
                "hij,hjk->hik", gram_mat, gram_mat, precision=lax.Precision.HIGHEST
            )
            poly_mat = COEF_B * gram_mat + COEF_C * square_mat
            updated.append(
                COEF_A * matrix
                + jnp.einsum("rhi,hij->rhj", matrix, poly_mat, precision=lax.Precision.HIGHEST)
            )
        current = tuple(updated)
    return current


def body(q_latent, kv_latent, q_cotangent, kv_cotangent):
    q_rows = q_latent.shape[1] // lax.axis_size("dp")
    kv_rows = kv_latent.shape[1] // lax.axis_size("dp")
    local_heads = q_cotangent.shape[1] // QDIM
    q_grad = lax.psum_scatter(
        latent_term(q_latent, q_cotangent), "dp", scatter_dimension=0, tiled=True
    )
    kv_grad = lax.psum_scatter(
        latent_term(kv_latent, kv_cotangent), "dp", scatter_dimension=0, tiled=True
    )
    q_blocks = q_grad.reshape(q_rows, local_heads, QDIM)
    kv_blocks = kv_grad.reshape(kv_rows, local_heads, KVDIM)

    def row_norms(values):
        return lax.psum(values, "dp")

    def row_grams(values):
        return lax.psum(values, "dp")

    q_final, kv_final = newton_schulz((q_blocks, kv_blocks), row_norms, row_grams)
    q_update = q_final.reshape(q_rows, local_heads * QDIM) * math.sqrt(QRANK)
    kv_update = kv_final.reshape(kv_rows, local_heads * KVDIM) * math.sqrt(KVRANK)
    return (q_update, kv_update)


def solution(mesh):
    return jax.shard_map(
        body,
        mesh=mesh,
        in_specs=(P("dp", None), P("dp", None), P("dp", "head"), P("dp", "head")),
        out_specs=(P("dp", "head"), P("dp", "head")),
        check_vma=False,
    )
```

profile of v0, /device:TPU:24, one launch (start us, length us, event | category | flops | bytes accessed | tf_op | source)
XLA Modules:
  0.0 1643.1 jit_solution(14685554945170208709)
XLA Ops:
  7.2 3.1 fusion.34
  10.4 2.8 fusion.29
  13.3 137.7 %reduce-scatter.5.cloned.1.call-done = f32[16,512]{1,0:T(8,128)} async-done(((f32[512,512]{1,0:T(8,128)}), f32[16,512]{1,0:T(8,128)}) %reduce-scatter.5.cloned.1.call-update) | async-done | bytes 32784 | tf_op jit(solution)/shard_map/reduce_scatter | solution.py:65
  151.0 0.8 multiply_reduce_fusion.1
  152.0 132.7 %reduce-scatter.3.cloned.1.call-done = f32[48,384]{1,0:T(8,128)} async-done(((f32[1536,384]{1,0:T(8,128)}), f32[48,384]{1,0:T(8,128)}) %reduce-scatter.3.cloned.1.call-update) | async-done | bytes 73744 | tf_op jit(solution)/shard_map/reduce_scatter | solution.py:62
  284.7 0.9 multiply_reduce_fusion
  285.8 61.1 %all-reduce = (f32[2]{0:T(128)S(1)}, f32[2]{0:T(128)S(1)}) all-reduce(f32[2]{0:T(128)S(1)} %reduce_sum.25, f32[2]{0:T(128)S(1)} %reduce_sum.37), channel_id=1, replica_groups=mesh['dp'=32,'head'=16] {'dp'}, use_global_device_ids=true, to_apply=%region_3.0 | all-reduce | flops 4 | bytes 32 | tf_op jit(solution)/shard_map/psum | solution.py:72
  346.9 2.3 fusion.26
  349.3 1.0 reshape.20
  350.3 1.3 fusion.23
  351.7 249.0 %all-reduce.20.cloned.1.call-done = (f32[2,192,192]{2,1,0:T(8,128)}, f32[2,256,256]{2,1,0:T(8,128)}) async-done(((f32[2,192,192]{2,1,0:T(8,128)}, f32[2,256,256]{2,1,0:T(8,128)}), (f32[2,192,192]{2,1,0:T(8,128)}, f32[2,256,256]{2,1,0:T(8,128)})) %all-reduce.20.cloned.1.call-update) | async-done | bytes 819216 | tf_op jit(solution)/shard_map/psum | solution.py:75
  600.7 2.3 fusion.4
  603.4 1.4 fusion.35
  605.8 1.2 fusion.30
  607.1 251.4 %all-reduce.18.cloned.1.call-done = (f32[2,192,192]{2,1,0:T(8,128)}, f32[2,256,256]{2,1,0:T(8,128)}) async-done(((f32[2,192,192]{2,1,0:T(8,128)}, f32[2,256,256]{2,1,0:T(8,128)}), (f32[2,192,192]{2,1,0:T(8,128)}, f32[2,256,256]{2,1,0:T(8,128)})) %all-reduce.18.cloned.1.call-update) | async-done | bytes 819216 | tf_op jit(solution)/shard_map/psum | solution.py:75
  858.5 2.3 fusion.3
  861.2 1.4 fusion.36
  862.6 0.5 fusion.8
  863.5 1.2 fusion.31
  864.8 251.4 %all-reduce.16.cloned.1.call-done = (f32[2,192,192]{2,1,0:T(8,128)}, f32[2,256,256]{2,1,0:T(8,128)}) async-done(((f32[2,192,192]{2,1,0:T(8,128)}, f32[2,256,256]{2,1,0:T(8,128)}), (f32[2,192,192]{2,1,0:T(8,128)}, f32[2,256,256]{2,1,0:T(8,128)})) %all-reduce.16.cloned.1.call-update) | async-done | bytes 819216 | tf_op jit(solution)/shard_map/psum | solution.py:75
  1116.2 2.3 fusion.2
  1118.9 1.4 fusion.37
  1121.3 1.2 fusion.32
  1122.8 250.8 %all-reduce.14.cloned.1.call-done = (f32[2,192,192]{2,1,0:T(8,128)}, f32[2,256,256]{2,1,0:T(8,128)}) async-done(((f32[2,192,192]{2,1,0:T(8,128)}, f32[2,256,256]{2,1,0:T(8,128)}), (f32[2,192,192]{2,1,0:T(8,128)}, f32[2,256,256]{2,1,0:T(8,128)})) %all-reduce.14.cloned.1.call-update) | async-done | bytes 819216 | tf_op jit(solution)/shard_map/psum | solution.py:75
  1373.5 2.3 fusion.1
  1376.2 1.4 fusion.38
  1377.6 0.5 fusion.6
  1378.5 1.2 fusion.33
  1379.8 251.4 %all-reduce.12.cloned.1.call-done = (f32[2,192,192]{2,1,0:T(8,128)}, f32[2,256,256]{2,1,0:T(8,128)}) async-done(((f32[2,192,192]{2,1,0:T(8,128)}, f32[2,256,256]{2,1,0:T(8,128)}), (f32[2,192,192]{2,1,0:T(8,128)}, f32[2,256,256]{2,1,0:T(8,128)})) %all-reduce.12.cloned.1.call-update) | async-done | bytes 819216 | tf_op jit(solution)/shard_map/psum | solution.py:75
  1631.2 2.3 fusion
  1633.9 0.6 copy.17
  1635.5 0.8 mul.152
  (49 shorter events, 6.5 us)
Async XLA Ops:
  7.2 3.2 copy-start
  7.2 3.2 copy-start.7
  7.2 143.8 %reduce-scatter.5.cloned.1.call-start = ((), (), s32[]{:S(2)}) async-start(), calls=%async_computation.3 | async-start | bytes 1081344 | tf_op jit(solution)/shard_map/reduce_scatter | solution.py:65
  10.4 274.4 %reduce-scatter.3.cloned.1.call-start = ((), (), s32[]{:S(2)}) async-start(), calls=%async_computation.2 | async-start | bytes 2433024 | tf_op jit(solution)/shard_map/reduce_scatter | solution.py:62
  13.3 587.4 %all-reduce.20.cloned.1.call-start = ((), (), s32[]{:S(2)}) async-start(), calls=%async_computation.8 | async-start | bytes 1835008 | tf_op jit(solution)/shard_map/psum | solution.py:75
  151.0 452.0 %copy-start.6 = (f32[16,512]{1,0:T(8,128)S(1)}, f32[16,512]{1,0:T(8,128)}, u32[]{:S(2)}) copy-start(f32[16,512]{1,0:T(8,128)} %reduce-scatter.5.cloned.1.call-done) | copy-start | bytes 98308
  351.6 506.9 %all-reduce.18.cloned.1.call-start = ((), (), s32[]{:S(2)}) async-start(), calls=%async_computation.7 | async-start | bytes 1835008 | tf_op jit(solution)/shard_map/psum | solution.py:75
  600.7 4.1 copy-start.1
  607.0 509.2 %all-reduce.16.cloned.1.call-start = ((), (), s32[]{:S(2)}) async-start(), calls=%async_computation.6 | async-start | bytes 1835008 | tf_op jit(solution)/shard_map/psum | solution.py:75
  858.5 4.1 copy-start.2
  864.8 508.7 %all-reduce.14.cloned.1.call-start = ((), (), s32[]{:S(2)}) async-start(), calls=%async_computation.5 | async-start | bytes 1835008 | tf_op jit(solution)/shard_map/psum | solution.py:75
  1116.2 4.1 copy-start.3
  1122.5 508.7 %all-reduce.12.cloned.1.call-start = ((), (), s32[]{:S(2)}) async-start(), calls=%async_computation.4 | async-start | bytes 1835008 | tf_op jit(solution)/shard_map/psum | solution.py:75
  1373.5 4.1 copy-start.4
  1631.2 3.3 copy-start.5
Sparse Core Ops, SparseCore 0:
  10.8 140.1 reduce-scatter.4
  154.1 130.6 reduce-scatter.2
  351.7 248.9 all-reduce.19
  607.1 251.3 all-reduce.17
  864.9 251.2 all-reduce.15
  1122.7 250.8 all-reduce.13
  1379.9 251.2 all-reduce.11
where the time goes:
time: 1640 us
  waiting for transfers between devices  1520 us (93%)
  blocking collectives  61.1 us (4%)
  matrix products  38.1 us (2%)
    psum x5, waiting for transfers between devices, row_grams(): return lax.psum(values, 'dp')  1250 us
    reduce_scatter x1, waiting for transfers between devices, body(): lax.psum_scatter(latent_term(kv_latent, kv_cotangent), 'dp', scatter_dime...  138 us
    reduce_scatter x1, waiting for transfers between devices, body(): lax.psum_scatter(latent_term(q_latent, q_cotangent), 'dp', scatter_dimens...  133 us
    psum x1, blocking collectives, row_norms(): return lax.psum(values, 'dp')  61.1 us
  transfers between devices with their start and end apart: 7, of which 7 were waited for; matrix products, arithmetic and copies ran while one was open for 0% of the time, Pallas kernels for 0%

commit v1 on v0

v1 whole, which is shorter than its diff:
```python
import functools
import math

import jax
import jax.numpy as jnp
from jax import lax
from jax.experimental import pallas as pl
from jax.experimental.pallas import tpu as pltpu
from jax.sharding import Mesh, PartitionSpec as P

QRANK = 1536
KVRANK = 512
QDIM = 192
KVDIM = 256
ITERS = 5
RESTART = 3

COEF_A = 3.4445
COEF_B = -4.775
COEF_C = 2.0315
EPSILON = 1e-06

LANES = 256
QTILES = QRANK // 2 // LANES
QPART = QTILES * QDIM
QUARTER = QPART + KVDIM
CUT = QUARTER // 2
GRAMS = QDIM + KVDIM
ZHIGH = 8
QOWN = QRANK // 32
KVOWN = KVRANK // 32
OWN = QOWN + KVOWN

PARAMS = pltpu.CompilerParams(vmem_limit_bytes=48 * 1024 * 1024)
VMEM = pl.BlockSpec(memory_space=pltpu.VMEM)
F32 = jnp.float32


def dot(lhs, rhs, dims):
    return lax.dot_general(
        lhs, rhs, (dims, ((), ())), precision=lax.Precision.HIGHEST, preferred_element_type=F32
    )


def mul(lhs, rhs):
    return dot(lhs, rhs, ((1,), (0,)))


def gradient_kernel(ql, kl, qc, kc, a_send, a_keep, b_send, b_keep):
    x, z = lax.axis_index("x"), lax.axis_index("zl")
    for away_h in (1, 0):
        second = (x ^ away_h) == 1
        qh = jnp.where(second, qc[:, QDIM:], qc[:, :QDIM])
        kh = jnp.where(second, kc[:, KVDIM:], kc[:, :KVDIM])
        a_out = a_send if away_h else a_keep
        for away_p in (1, 0):
            half = z ^ away_p
            b_out = b_send if away_p else b_keep
            for tile in range(QTILES):
                start = pl.multiple_of(half * (QRANK // 2) + tile * LANES, LANES)
                part = lax.dot_general(
                    qh, ql[:, pl.ds(start, LANES)], (((0,), (0,)), ((), ())), preferred_element_type=F32
                )
                low = tile * QDIM
                inside = min(max(CUT - low, 0), QDIM)
                if inside:
                    a_out[away_p, low : low + inside, :] = part[:inside]
                if inside < QDIM:
                    b_out[away_h, low + inside - CUT : low + QDIM - CUT, :] = part[inside:]
            start = pl.multiple_of(half * LANES, LANES)
            part = lax.dot_general(
                kh, kl[:, pl.ds(start, LANES)], (((0,), (0,)), ((), ())), preferred_element_type=F32
            )
            b_out[away_h, QPART - CUT :, :] = part


def put_grams(out, q_tiles, kv):
    q_gram = sum(dot(tile, tile, ((1,), (1,))) for tile in q_tiles)
    out[:QDIM, :QDIM] = q_gram
    out[:QDIM, QDIM:] = jnp.zeros((QDIM, LANES - QDIM), F32)
    out[QDIM:, :] = dot(kv, kv, ((1,), (1,)))


def gram_kernel(y, out):
    put_grams(out, [y[t * QDIM : (t + 1) * QDIM, :] for t in range(QTILES)], y[QPART:, :])


def identity(size):
    rows = lax.broadcasted_iota(jnp.int32, (size, size), 0)
    return rows == lax.broadcasted_iota(jnp.int32, (size, size), 1)


def steps(grams, count):
    products = [None] * len(grams)
    for index in range(count):
        squares = [mul(gram, gram) for gram in grams]
        polys = [COEF_B * gram + COEF_C * square for gram, square in zip(grams, squares)]
        for k, poly in enumerate(polys):
            if products[k] is None:
                products[k] = jnp.where(identity(poly.shape[0]), COEF_A + poly, poly)
            else:
                products[k] = COEF_A * products[k] + mul(products[k], poly)
        if index + 1 < count:
            inner = [COEF_A * gram + mul(gram, poly) for gram, poly in zip(grams, polys)]
            grams = [COEF_A * mid + mul(poly, mid) for mid, poly in zip(inner, polys)]
    return products


def first_kernel(mine, other, y, x_out, out):
    total = mine[...] + other[...]
    q_gram, kv_gram = total[:QDIM, :QDIM], total[QDIM:, :]
    grams, scales = [], []
    for gram in (q_gram, kv_gram):
        trace = jnp.sum(jnp.where(identity(gram.shape[0]), gram, 0.0))
        scale = lax.rsqrt(jnp.full((1, LANES), trace + EPSILON, F32))
        scales.append(scale)
        wide = scale[:, : gram.shape[0]]
        grams.append(gram * wide * wide)
    q_prod, kv_prod = steps(grams, RESTART)
    tiles = []
    for t in range(QTILES):
        rows = slice(t * QDIM, (t + 1) * QDIM)
        tile = mul(q_prod, y[rows, :] * scales[0])
        x_out[rows, :] = tile
        tiles.append(tile)
    kv = mul(kv_prod, y[QPART:, :] * scales[1])
    x_out[QPART:, :] = kv
    put_grams(out, tiles, kv)


def second_kernel(mine, other, xt, out, q_scratch, kv_scratch):
    total = mine[...] + other[...]
    q_prod, kv_prod = steps([total[:QDIM, :QDIM], total[QDIM:, :]], ITERS - RESTART)
    for t in range(QTILES):
        q_scratch[t * LANES : (t + 1) * LANES, :] = dot(xt[t * QDIM : (t + 1) * QDIM, :], q_prod, ((0,), (0,)))
    kv_scratch[...] = dot(xt[QPART:, :], kv_prod, ((0,), (0,)))
    high = lax.axis_index("zh")
    for k in range(2):
        q_start = pl.multiple_of(high * (2 * QOWN) + k * QOWN, 8)
        kv_start = pl.multiple_of(high * (2 * KVOWN) + k * KVOWN, 8)
        q_rows = q_scratch[pl.ds(q_start, QOWN), :] * math.sqrt(QRANK)
        kv_rows = kv_scratch[pl.ds(kv_start, KVOWN), :] * math.sqrt(KVRANK)
        for owner in range(2):
            out[2 * owner + k, :QOWN, :QDIM] = q_rows
            out[2 * owner + k, :QOWN, QDIM:] = jnp.zeros((QOWN, LANES - QDIM), F32)
            out[2 * owner + k, QOWN:, :] = kv_rows


def join_kernel(got, q_out, kv_out):
    x = lax.axis_index("x")
    for head in range(2):
        block = got[2 * head + x]
        q_out[:, head * QDIM : (head + 1) * QDIM] = block[:QOWN, :QDIM]
        kv_out[:, head * KVDIM : (head + 1) * KVDIM] = block[QOWN:, :]


def shape(*dims):
    return jax.ShapeDtypeStruct(dims, F32)


def call(kernel, outs, inputs, scratch=()):
    single = not isinstance(outs, tuple)
    return pl.pallas_call(
        kernel,
        out_shape=outs,
        in_specs=[VMEM] * inputs,
        out_specs=VMEM if single else (VMEM,) * len(outs),
        scratch_shapes=list(scratch),
        compiler_params=PARAMS,
    )


PAIR = [(0, 1), (1, 0)]


def body(q_latent, kv_latent, q_cotangent, kv_cotangent):
    half = shape(2, CUT, LANES)
    a_send, a_keep, b_send, b_keep = call(gradient_kernel, (half,) * 4, 4)(
        q_latent, kv_latent, q_cotangent, kv_cotangent
    )
    a_got = lax.ppermute(a_send, "x", PAIR)
    b_got = lax.ppermute(b_send, "zl", PAIR)
    a_next = lax.ppermute(a_keep[1] + a_got[1], "zl", PAIR)
    b_next = lax.ppermute(b_keep[1] + b_got[1], "x", PAIR)
    quarter = jnp.concatenate((a_keep[0] + a_got[0] + a_next, b_keep[0] + b_got[0] + b_next), axis=0)
    spread = lax.all_to_all(quarter.reshape(ZHIGH, QUARTER // ZHIGH, LANES), "zh", 0, 0)
    y = lax.all_gather(jnp.sum(spread, axis=0), "zh", axis=0, tiled=True)
    grams = shape(GRAMS, LANES)
    mine = call(gram_kernel, grams, 1)(y)
    other = lax.ppermute(mine, "zl", PAIR)
    xt, mine = call(first_kernel, (shape(QUARTER, LANES), grams), 3)(mine, other, y)
    other = lax.ppermute(mine, "zl", PAIR)
    ready = call(
        second_kernel,
        shape(4, OWN, LANES),
        3,
        (pltpu.VMEM((QRANK // 2, QDIM), F32), pltpu.VMEM((KVRANK // 2, KVDIM), F32)),
    )(mine, other, xt)
    got = lax.all_to_all(ready, ("x", "zl"), 0, 0)
    return call(join_kernel, (shape(QOWN, 2 * QDIM), shape(KVOWN, 2 * KVDIM)), 1)(got)


def solution(mesh):
    fine = Mesh(mesh.devices.reshape(2, ZHIGH, 2, -1), ("x", "zh", "zl", "head"))
    rows = ("x", "zh", "zl")
    return jax.shard_map(
        body,
        mesh=fine,
        in_specs=(P(rows, None), P(rows, None), P(rows, "head"), P(rows, "head")),
        out_specs=(P(rows, "head"), P(rows, "head")),
        check_vma=False,
    )
```

time: 1640 us -> 179 us (0.11)
  waiting for transfers between devices: 1520 us -> 40.9 us
  matrix products: 38.1 us -> 0 us
  blocking collectives: 61.1 us -> 98.3 us
  starting transfers between devices: 0.47 us -> 18.4 us
    psum x5 -> x0, waiting for transfers between devices: 1250 us -> none  [row_grams(): return lax.psum(values, 'dp')]
    reduce_scatter x2 -> x0, waiting for transfers between devices: 270 us -> none  [the longest x1 138 us: body(): lax.psum_scatter(latent_term(kv_latent, kv_cotangent), 'dp', scatter_dime...]
    all_to_all x0 -> x2, blocking collectives: none -> 67 us  [the longest x1 58.9 us: body(): lax.all_to_all(quarter.reshape(ZHIGH, QUARTER // ZHIGH, LANES), 'zh', 0, 0)]
    psum x1 -> x0, blocking collectives: 61.1 us -> none  [row_norms(): return lax.psum(values, 'dp')]
    ppermute x0 -> x6, waiting for transfers between devices: none -> 40.9 us  [the longest x2 16.7 us: body(): other = lax.ppermute(mine, 'zl', PAIR)]
    dot_general x32 -> x0, matrix products: 38.1 us -> none  [the longest x10 14.3 us: newton_schulz(): jnp.einsum('rhi,rhj->hij', matrix, matrix, precision=lax.Precision.HIGHEST)]
    all_gather x0 -> x1, blocking collectives: none -> 31.3 us  [body(): y = lax.all_gather(jnp.sum(spread, axis=0), 'zh', axis=0, tiled=True)]
    ppermute x0 -> x6, starting transfers between devices: none -> 18.4 us  [the longest x2 4.02 us: body(): other = lax.ppermute(mine, 'zl', PAIR)]
  transfers between devices with their start and end apart: 7 -> 6, of which waited for: 7 -> 5; matrix products, arithmetic and copies ran while one was open for 0% -> 0% of each run, Pallas kernels for 0% -> 0%
where the time goes in v1:
time: 179 us; the launch traced here: 177 us
  blocking collectives  98.3 us (55%)
  waiting for transfers between devices  40.9 us (23%)
  starting transfers between devices  18.4 us (10%)
  Pallas kernels  15.3 us (9%)
  local copies, waits for them, and re-layouts  3.32 us (2%)
    all_to_all x1, blocking collectives, body(): lax.all_to_all(quarter.reshape(ZHIGH, QUARTER // ZHIGH, LANES), 'zh', 0, 0)  58.9 us
    all_gather x1, blocking collectives, body(): y = lax.all_gather(jnp.sum(spread, axis=0), 'zh', axis=0, tiled=True)  31.3 us
    ppermute x2, waiting for transfers between devices, body(): other = lax.ppermute(mine, 'zl', PAIR)  16.7 us
    ppermute x1, waiting for transfers between devices, body(): a_got = lax.ppermute(a_send, 'x', PAIR)  15.4 us
    all_to_all x1, blocking collectives, body(): got = lax.all_to_all(ready, ('x', 'zl'), 0, 0)  8.11 us
    pallas_call x1, Pallas kernels, body(): call(first_kernel, (shape(QUARTER, LANES), grams), 3)(mine, other, y)  6.19 us
    ppermute x1, waiting for transfers between devices, body(): a_next = lax.ppermute(a_keep[1] + a_got[1], 'zl', PAIR)  5.44 us
    ppermute x2, starting transfers between devices, body(): other = lax.ppermute(mine, 'zl', PAIR)  4.02 us
  transfers between devices with their start and end apart: 6, of which 5 were waited for; matrix products, arithmetic and copies ran while one was open for 0% of the time, Pallas kernels for 0%

profile of v1, /device:TPU:24, one launch (start us, length us, event | category | flops | bytes accessed | tf_op | source)
XLA Modules:
  0.0 177.3 jit_solution(12153038972176288287)
XLA Ops:
  0.6 0.0 copy-start
  0.6 1.1 copy-done
  1.8 0.0 copy-start.1
  1.8 1.1 copy-done.1
  2.9 0.0 copy-start.2
  2.9 1.1 copy-done.2
  4.0 3.8 %shard_map.59 = (f32[2,416,256]{2,1,0:T(8,128)S(1)}, f32[2,416,256]{2,1,0:T(8,128)S(1)}, f32[2,416,256]{2,1,0:T(8,128)S(1)}, f32[2,416,256]{2,1,0:T(8,128)S(1)}) custom-call(bf16[768,1536]{1,0:T(8,128)(2,1)} %ql.1, bf16[768,512]{1,0:T(8,128)(2,1)S(1)} %copy-done, bf16[768,384]{1,0:T(8,128)(2,1)S(1)} %copy-done.2, bf16[768,512]{1,0:T(8,128)(2,1)S(1)} %copy-done.1), custom_call_target="tpu_custom_call" | custom-call | tf_op jit(solution)/shard_map/pallas_call | solution.py:178
  7.8 3.4 %collective-permute-start = (f32[2,416,256]{2,1,0:T(8,128)S(1)}, f32[2,416,256]{2,1,0:T(8,128)S(1)}, u32[]{:S(2)}, u32[]{:S(2)}) collective-permute-start(f32[2,416,256]{2,1,0:T(8,128)S(1)} %get-tuple-element.9), channel_id=1, source_target_pairs={{0,256},{256,0},{1,257},{257,1},{2,258},{258,2},{3,259},{259,3},{4... | collective-permute-start | bytes 2555912 | tf_op jit(solution)/shard_map/ppermute | solution.py:181
  11.2 3.8 %collective-permute-start.2 = (f32[2,416,256]{2,1,0:T(8,128)S(1)}, f32[2,416,256]{2,1,0:T(8,128)S(1)}, u32[]{:S(2)}, u32[]{:S(2)}) collective-permute-start(f32[2,416,256]{2,1,0:T(8,128)S(1)} %get-tuple-element.11), channel_id=1, source_target_pairs={{0,16},{16,0},{1,17},{17,1},{2,18},{18,2},{3,19},{19,3},{4,20},{20... | collective-permute-start | bytes 2555912 | tf_op jit(solution)/shard_map/ppermute | solution.py:182
  15.0 15.4 %collective-permute-done = f32[2,416,256]{2,1,0:T(8,128)S(1)} collective-permute-done((f32[2,416,256]{2,1,0:T(8,128)S(1)}, f32[2,416,256]{2,1,0:T(8,128)S(1)}, u32[]{:S(2)}, u32[]{:S(2)}) %collective-permute-start) | collective-permute-done | bytes 852000 | tf_op jit(solution)/shard_map/ppermute | solution.py:181
  30.4 0.1 fusion.3
  30.4 3.8 %collective-permute-start.1 = (f32[416,256]{1,0:T(8,128)S(1)}, f32[416,256]{1,0:T(8,128)S(1)}, u32[]{:S(2)}, u32[]{:S(2)}) collective-permute-start(f32[416,256]{1,0:T(8,128)S(1)} %fusion.3), channel_id=1, source_target_pairs={{0,16},{16,0},{1,17},{17,1},{2,18},{18,2},{3,19},{19,3},{4,20},{20... | collective-permute-start | bytes 1277960 | tf_op jit(solution)/shard_map/ppermute | solution.py:183
  34.2 0.0 collective-permute-done.2
  34.2 0.1 fusion
  34.3 3.4 %collective-permute-start.3 = (f32[416,256]{1,0:T(8,128)S(1)}, f32[416,256]{1,0:T(8,128)S(1)}, u32[]{:S(2)}, u32[]{:S(2)}) collective-permute-start(f32[416,256]{1,0:T(8,128)S(1)} %fusion), channel_id=1, source_target_pairs={{0,256},{256,0},{1,257},{257,1},{2,258},{258,2},{3,259},{259,3},{4... | collective-permute-start | bytes 1277960 | tf_op jit(solution)/shard_map/ppermute | solution.py:184
  37.7 5.4 %collective-permute-done.1 = f32[416,256]{1,0:T(8,128)S(1)} collective-permute-done((f32[416,256]{1,0:T(8,128)S(1)}, f32[416,256]{1,0:T(8,128)S(1)}, u32[]{:S(2)}, u32[]{:S(2)}) %collective-permute-start.1) | collective-permute-done | bytes 426016 | tf_op jit(solution)/shard_map/ppermute | solution.py:183
  43.2 0.1 fusion.5
  43.2 3.4 %collective-permute-done.3 = f32[416,256]{1,0:T(8,128)S(1)} collective-permute-done((f32[416,256]{1,0:T(8,128)S(1)}, f32[416,256]{1,0:T(8,128)S(1)}, u32[]{:S(2)}, u32[]{:S(2)}) %collective-permute-start.3) | collective-permute-done | bytes 426016 | tf_op jit(solution)/shard_map/ppermute | solution.py:184
  46.6 0.1 fusion.2
  46.7 0.1 pad_maximum_fusion
  46.8 58.9 %all_to_all.10 = f32[8,104,256]{2,1,0:T(8,128)S(1)} all-to-all(f32[8,104,256]{2,1,0:T(8,128)S(1)} %bitcast.13), channel_id=1, replica_groups=mesh['x'=2,'zh'=8,'zl'=2,'head'=16] {'zh'}, dimensions={0} | all-to-all | bytes 1703936 | tf_op jit(solution)/shard_map/all_to_all | solution.py:186
  105.6 0.1 reduce_sum.9
  105.7 31.3 %all_gather.3.y = f32[832,256]{1,0:T(8,128)S(1)} all-gather(f32[104,256]{1,0:T(8,128)S(1)} %reduce_sum.9), channel_id=1, replica_groups=mesh['x'=2,'zh'=8,'zl'=2,'head'=16] {'zh'}, dimensions={0}, use_global_device_ids=true | all-gather | bytes 958464 | tf_op jit(solution)/shard_map/all_gather | solution.py:187
  137.0 0.9 shard_map.60.mine
  137.9 1.9 %collective-permute-start.4 = (f32[448,256]{1,0:T(8,128)S(1)}, f32[448,256]{1,0:T(8,128)S(1)}, u32[]{:S(2)}, u32[]{:S(2)}) collective-permute-start(f32[448,256]{1,0:T(8,128)S(1)} %shard_map.60.mine), channel_id=1, source_target_pairs={{0,16},{16,0},{1,17},{17,1},{2,18},{18,2},{3,19},{19,3},{4,20},{20... | collective-permute-start | bytes 1376264 | tf_op jit(solution)/shard_map/ppermute | solution.py:190
  139.8 8.4 %collective-permute-done.4.other = f32[448,256]{1,0:T(8,128)S(1)} collective-permute-done((f32[448,256]{1,0:T(8,128)S(1)}, f32[448,256]{1,0:T(8,128)S(1)}, u32[]{:S(2)}, u32[]{:S(2)}) %collective-permute-start.4) | collective-permute-done | bytes 458784 | tf_op jit(solution)/shard_map/ppermute | solution.py:190
  148.2 6.2 %shard_map.61 = (f32[832,256]{1,0:T(8,128)S(1)}, f32[448,256]{1,0:T(8,128)S(1)}) custom-call(f32[448,256]{1,0:T(8,128)S(1)} %shard_map.60.mine, f32[448,256]{1,0:T(8,128)S(1)} %collective-permute-done.4.other, f32[832,256]{1,0:T(8,128)S(1)} %all_gather.3.y), custom_call_target="tpu_custom_call" | custom-call | tf_op jit(solution)/shard_map/pallas_call | solution.py:191
  154.4 2.1 %collective-permute-start.5 = (f32[448,256]{1,0:T(8,128)S(1)}, f32[448,256]{1,0:T(8,128)S(1)}, u32[]{:S(2)}, u32[]{:S(2)}) collective-permute-start(f32[448,256]{1,0:T(8,128)S(1)} %get-tuple-element.12.mine), channel_id=1, source_target_pairs={{0,16},{16,0},{1,17},{17,1},{2,18},{18,2},{3,19},{19,3},{4,20},{20... | collective-permute-start | bytes 1376264 | tf_op jit(solution)/shard_map/ppermute | solution.py:192
  156.5 8.3 %collective-permute-done.5.other = f32[448,256]{1,0:T(8,128)S(1)} collective-permute-done((f32[448,256]{1,0:T(8,128)S(1)}, f32[448,256]{1,0:T(8,128)S(1)}, u32[]{:S(2)}, u32[]{:S(2)}) %collective-permute-start.5) | collective-permute-done | bytes 458784 | tf_op jit(solution)/shard_map/ppermute | solution.py:192
  164.8 3.7 %shard_map.62 = f32[4,64,256]{2,1,0:T(8,128)S(1)} custom-call(f32[448,256]{1,0:T(8,128)S(1)} %get-tuple-element.12.mine, f32[448,256]{1,0:T(8,128)S(1)} %collective-permute-done.5.other, f32[832,256]{1,0:T(8,128)S(1)} %get-tuple-element.13.xt), custom_call_target="tpu_custom_call" | custom-call | tf_op jit(solution)/shard_map/pallas_call | solution.py:193
  168.5 8.1 %all_to_all.11.got = f32[4,64,256]{2,1,0:T(8,128)S(1)} all-to-all(f32[4,64,256]{2,1,0:T(8,128)S(1)} %shard_map.62), channel_id=1, replica_groups=mesh['x'=2,'zh'=8,'zl'=2,'head'=16] {'x','zl'}, dimensions={0} | all-to-all | bytes 524288 | tf_op jit(solution)/shard_map/all_to_all | solution.py:199
  176.6 0.7 shard_map.63
Async XLA Ops:
  0.6 1.1 copy-start
  1.8 1.1 copy-start.1
  2.9 1.1 copy-start.2
  7.8 22.6 %collective-permute-start = (f32[2,416,256]{2,1,0:T(8,128)S(1)}, f32[2,416,256]{2,1,0:T(8,128)S(1)}, u32[]{:S(2)}, u32[]{:S(2)}) collective-permute-start(f32[2,416,256]{2,1,0:T(8,128)S(1)} %get-tuple-element.9), channel_id=1, source_target_pairs={{0,256},{256,0},{1,257},{257,1},{2,258},{258,2},{3,259},{259,3},{4... | collective-permute-start | bytes 2555912 | tf_op jit(solution)/shard_map/ppermute | solution.py:181
  11.2 23.0 %collective-permute-start.2 = (f32[2,416,256]{2,1,0:T(8,128)S(1)}, f32[2,416,256]{2,1,0:T(8,128)S(1)}, u32[]{:S(2)}, u32[]{:S(2)}) collective-permute-start(f32[2,416,256]{2,1,0:T(8,128)S(1)} %get-tuple-element.11), channel_id=1, source_target_pairs={{0,16},{16,0},{1,17},{17,1},{2,18},{18,2},{3,19},{19,3},{4,20},{20... | collective-permute-start | bytes 2555912 | tf_op jit(solution)/shard_map/ppermute | solution.py:182
  30.4 12.7 %collective-permute-start.1 = (f32[416,256]{1,0:T(8,128)S(1)}, f32[416,256]{1,0:T(8,128)S(1)}, u32[]{:S(2)}, u32[]{:S(2)}) collective-permute-start(f32[416,256]{1,0:T(8,128)S(1)} %fusion.3), channel_id=1, source_target_pairs={{0,16},{16,0},{1,17},{17,1},{2,18},{18,2},{3,19},{19,3},{4,20},{20... | collective-permute-start | bytes 1277960 | tf_op jit(solution)/shard_map/ppermute | solution.py:183
  34.3 12.3 %collective-permute-start.3 = (f32[416,256]{1,0:T(8,128)S(1)}, f32[416,256]{1,0:T(8,128)S(1)}, u32[]{:S(2)}, u32[]{:S(2)}) collective-permute-start(f32[416,256]{1,0:T(8,128)S(1)} %fusion), channel_id=1, source_target_pairs={{0,256},{256,0},{1,257},{257,1},{2,258},{258,2},{3,259},{259,3},{4... | collective-permute-start | bytes 1277960 | tf_op jit(solution)/shard_map/ppermute | solution.py:184
  137.9 10.4 %collective-permute-start.4 = (f32[448,256]{1,0:T(8,128)S(1)}, f32[448,256]{1,0:T(8,128)S(1)}, u32[]{:S(2)}, u32[]{:S(2)}) collective-permute-start(f32[448,256]{1,0:T(8,128)S(1)} %shard_map.60.mine), channel_id=1, source_target_pairs={{0,16},{16,0},{1,17},{17,1},{2,18},{18,2},{3,19},{19,3},{4,20},{20... | collective-permute-start | bytes 1376264 | tf_op jit(solution)/shard_map/ppermute | solution.py:190
  154.4 10.4 %collective-permute-start.5 = (f32[448,256]{1,0:T(8,128)S(1)}, f32[448,256]{1,0:T(8,128)S(1)}, u32[]{:S(2)}, u32[]{:S(2)}) collective-permute-start(f32[448,256]{1,0:T(8,128)S(1)} %get-tuple-element.12.mine), channel_id=1, source_target_pairs={{0,16},{16,0},{1,17},{17,1},{2,18},{18,2},{3,19},{19,3},{4,20},{20... | collective-permute-start | bytes 1376264 | tf_op jit(solution)/shard_map/ppermute | solution.py:192

commit v2 on v0

v2 whole, which is shorter than its diff:
```python
import math

import jax
import jax.numpy as jnp
from jax import lax
from jax.experimental import pallas as pl
from jax.experimental.pallas import tpu as pltpu
from jax.sharding import Mesh, PartitionSpec as P

QRANK = 1536
KVRANK = 512
QDIM = 192
KVDIM = 256
ITERS = 5
RESTART = 3

COEF_A = 3.4445
COEF_B = -4.775
COEF_C = 2.0315
EPSILON = 1e-06

LANES = 256
QTILES = QRANK // 2 // LANES
QPART = QTILES * QDIM
QUARTER = QPART + KVDIM
CUT = QUARTER // 2
ZHIGH = 8
USED = QUARTER // ZHIGH
SHARD = USED + 7
QOWN = QRANK // 32
KVOWN = KVRANK // 32

MEBI = 1024 * 1024
VMEM = pl.BlockSpec(memory_space=pltpu.VMEM)
F32 = jnp.float32


def dot(lhs, rhs, dims):
    return lax.dot_general(
        lhs, rhs, (dims, ((), ())), precision=lax.Precision.HIGHEST, preferred_element_type=F32
    )


def mul(lhs, rhs):
    return dot(lhs, rhs, ((1,), (0,)))


def products(cot, start, stop, lat):
    return lax.dot_general(
        cot[:, start:stop], lat, (((0,), (0,)), ((), ())), preferred_element_type=F32
    )


def fill(q_cot, kv_cot, q_lat, kv_lat, a_out, b_out):
    for tile in range(QTILES):
        lat = q_lat(tile)
        low = tile * QDIM
        inside = min(max(CUT - low, 0), QDIM)
        if inside and a_out is not None:
            a_out[low : low + inside, :] = products(q_cot, 0, inside, lat)
        if inside < QDIM and b_out is not None:
            b_out[low + inside - CUT : low + QDIM - CUT, :] = products(q_cot, inside, QDIM, lat)
    if b_out is not None:
        b_out[QPART - CUT :, :] = products(kv_cot, 0, KVDIM, kv_lat)


def heads(qc, kc, x, away):
    second = (x ^ away) == 1
    q_cot = jnp.where(second, qc[:, QDIM:], qc[:, :QDIM])
    return q_cot, jnp.where(second, kc[:, KVDIM:], kc[:, :KVDIM])


def send_kernel(ql, kl, qc, kc, a_send, b_send, qc_v, kc_v, ql_v, kl_v, sems):
    x, z = lax.axis_index("x"), lax.axis_index("zl")
    q_half, kv_half = QRANK // 2, KVRANK // 2
    copies = [pltpu.make_async_copy(qc, qc_v, sems.at[0])]
    for away in (1, 0):
        lanes = pl.ds(pl.multiple_of((z ^ away) * q_half, LANES), q_half)
        copies.append(pltpu.make_async_copy(ql.at[:, lanes], ql_v.at[away], sems.at[2 - away]))
    lanes = pl.ds(pl.multiple_of((z ^ 1) * kv_half, LANES), kv_half)
    copies.append(pltpu.make_async_copy(kc, kc_v, sems.at[3]))
    copies.append(pltpu.make_async_copy(kl.at[:, lanes], kl_v, sems.at[4]))
    for copy in copies:
        copy.start()

    def q_lat(away):
        return lambda tile: ql_v[away, :, tile * LANES : (tile + 1) * LANES]

    copies[0].wait()
    copies[1].wait()
    q_cot = jnp.where((x ^ 1) == 1, qc_v[:, QDIM:], qc_v[:, :QDIM])
    fill(q_cot, None, q_lat(1), None, a_send.at[1], None)
    copies[2].wait()
    fill(q_cot, None, q_lat(0), None, a_send.at[0], None)
    copies[3].wait()
    copies[4].wait()
    for away in (1, 0):
        q_cot, kv_cot = heads(qc_v, kc_v, x, away)
        fill(q_cot, kv_cot, q_lat(1), kl_v[...], None, b_send.at[away])


def keep_kernel(ql, kl, qc, kc, a_keep, b_keep, qc_v, kc_v, ql_v, kl_v, sems):
    x, z = lax.axis_index("x"), lax.axis_index("zl")
    q_half, kv_half = QRANK // 2, KVRANK // 2
    lanes = pl.ds(pl.multiple_of(z * kv_half, LANES), kv_half)
    copies = [
        pltpu.make_async_copy(qc, qc_v, sems.at[0]),
        pltpu.make_async_copy(kc, kc_v, sems.at[1]),
        pltpu.make_async_copy(kl.at[:, lanes], kl_v, sems.at[2]),
    ]
    for away in (0, 1):
        lanes = pl.ds(pl.multiple_of((z ^ away) * q_half, LANES), q_half)
        copies.append(pltpu.make_async_copy(ql.at[:, lanes], ql_v.at[away], sems.at[3 + away]))
    for copy in copies:
        copy.start()
    for copy in copies:
        copy.wait()

    def q_lat(away):
        return lambda tile: ql_v[away, :, tile * LANES : (tile + 1) * LANES]

    q_cot, kv_cot = heads(qc_v, kc_v, x, 1)
    fill(q_cot, kv_cot, q_lat(0), kl_v[...], None, b_keep.at[1])
    q_cot, kv_cot = heads(qc_v, kc_v, x, 0)
    fill(q_cot, kv_cot, q_lat(1), None, a_keep.at[1], None)
    fill(q_cot, kv_cot, q_lat(0), kl_v[...], a_keep.at[0], b_keep.at[0])


def place_kernel(a_keep, a_got, a_next, b_keep, b_got, b_next, out):
    for index in range(ZHIGH):
        for keep, got, last, low in ((a_keep, a_got, a_next, 0), (b_keep, b_got, b_next, CUT)):
            start, stop = max(index * USED, low), min((index + 1) * USED, low + CUT)
            if start < stop:
                rows = slice(start - low, stop - low)
                where = index * SHARD + start - index * USED
                out[where : where + stop - start, :] = keep[0, rows, :] + got[0, rows, :] + last[rows, :]
        out[index * SHARD + USED : (index + 1) * SHARD, :] = jnp.zeros((SHARD - USED, LANES), F32)


def identity(size):
    rows = lax.broadcasted_iota(jnp.int32, (size, size), 0)
    return rows == lax.broadcasted_iota(jnp.int32, (size, size), 1)


def steps(gram, count):
    product = None
    for index in range(count):
        poly = COEF_B * gram + COEF_C * mul(gram, gram)
        if product is None:
            product = jnp.where(identity(poly.shape[0]), COEF_A + poly, poly)
        else:
            product = COEF_A * product + mul(product, poly)
        if index + 1 < count:
            inner = COEF_A * gram + mul(gram, poly)
            gram = COEF_A * inner + mul(poly, inner)
    return product


def orthogonalize(tiles, norm, rows):
    gram = sum(dot(tile, tile, ((1,), (1,))) for tile in tiles)
    size = gram.shape[0]
    trace = jnp.sum(jnp.where(identity(size), gram, 0.0))
    scale = lax.rsqrt(jnp.full((1, LANES), trace + EPSILON, F32))
    wide = scale[:, :size]
    product = steps(gram * wide * wide, RESTART)
    tiles = [mul(product, tile * scale) for tile in tiles]
    gram = sum(dot(tile, tile, ((1,), (1,))) for tile in tiles)
    product = steps(gram, ITERS - RESTART)
    for index, tile in enumerate(tiles):
        rows[index * LANES : (index + 1) * LANES, :] = dot(tile, product, ((0,), (0,))) * norm


def update_kernel(y, q_other, kv_other, out, q_rows, kv_rows):
    z, high = lax.axis_index("zl"), lax.axis_index("zh")

    def q_tiles(ref):
        return [ref[t * QDIM : (t + 1) * QDIM, :] for t in range(QTILES)]

    @pl.when(z == 0)
    def _():
        orthogonalize(q_tiles(y) + q_tiles(q_other), math.sqrt(QRANK), q_rows)
        for half in range(2):
            for k in range(2):
                start = pl.multiple_of(half * (QRANK // 2) + (2 * high + k) * QOWN, 8)
                out[2 * half + k, :, :QDIM] = q_rows[pl.ds(start, QOWN), :]
                out[2 * half + k, :, QDIM:] = jnp.zeros((QOWN, LANES - QDIM), F32)

    @pl.when(z == 1)
    def _():
        orthogonalize([kv_other[...], y[QPART:, :]], math.sqrt(KVRANK), kv_rows)
        for half in range(2):
            for k in range(2):
                start = pl.multiple_of(half * (KVRANK // 2) + (2 * high + k) * KVOWN, 8)
                out[2 * half + k, :KVOWN, :] = kv_rows[pl.ds(start, KVOWN), :]
                out[2 * half + k, KVOWN:, :] = jnp.zeros((QOWN - KVOWN, LANES), F32)


def join_kernel(got, q_out, kv_out):
    for head in range(2):
        q_out[:, head * QDIM : (head + 1) * QDIM] = got[2 * head, :, :QDIM]
        kv_out[:, head * KVDIM : (head + 1) * KVDIM] = got[2 * head + 1, :KVOWN, :]


def shape(*dims):
    return jax.ShapeDtypeStruct(dims, F32)


def call(kernel, outs, inputs, scratch=(), space=pltpu.VMEM, cost=None, vmem=24):
    single = not isinstance(outs, tuple)
    return pl.pallas_call(
        kernel,
        out_shape=outs,
        in_specs=[pl.BlockSpec(memory_space=space)] * inputs,
        out_specs=VMEM if single else (VMEM,) * len(outs),
        scratch_shapes=list(scratch),
        compiler_params=pltpu.CompilerParams(vmem_limit_bytes=vmem * MEBI),
        cost_estimate=cost,
    )


PAIR = [(0, 1), (1, 0)]


def body(q_latent, kv_latent, q_cotangent, kv_cotangent):
    half = shape(2, CUT, LANES)
    tokens = q_latent.shape[0]
    scratch = [
        pltpu.VMEM(dims, q_latent.dtype)
        for dims in (q_cotangent.shape, kv_cotangent.shape, (2, tokens, QRANK // 2), (tokens, KVRANK // 2))
    ]
    scratch.append(pltpu.SemaphoreType.DMA((5,)))
    args = (q_latent, kv_latent, q_cotangent, kv_cotangent)
    cost = pl.CostEstimate(flops=2 * tokens * 2 * 2 * CUT * LANES, bytes_accessed=8 << 20, transcendentals=0)
    a_send, b_send = call(send_kernel, (half, half), 4, scratch, pltpu.HBM, cost, 60)(*args)
    a_got = lax.ppermute(a_send, "x", PAIR)
    b_got = lax.ppermute(b_send, "zl", PAIR)
    a_keep, b_keep = call(keep_kernel, (half, half), 4, scratch, pltpu.HBM, cost, 60)(*args)
    a_next = lax.ppermute(a_keep[1] + a_got[1], "zl", PAIR)
    b_next = lax.ppermute(b_keep[1] + b_got[1], "x", PAIR)
    placed = call(place_kernel, shape(ZHIGH * SHARD, LANES), 6)(a_keep, a_got, a_next, b_keep, b_got, b_next)
    part = lax.optimization_barrier(lax.psum_scatter(placed, "zh", scatter_dimension=0, tiled=True))
    y = lax.all_gather(part[:USED], "zh", axis=0, tiled=True)
    q_other = lax.ppermute(y[:QPART], "zl", [(1, 0)])
    kv_other = lax.ppermute(y[QPART:], "zl", [(0, 1)])
    rows = (pltpu.VMEM((QRANK, QDIM), F32), pltpu.VMEM((KVRANK, KVDIM), F32))
    ready = call(update_kernel, shape(4, QOWN, LANES), 3, rows)(y, q_other, kv_other)
    got = lax.all_to_all(ready, ("x", "zl"), 0, 0)
    return call(join_kernel, (shape(QOWN, 2 * QDIM), shape(KVOWN, 2 * KVDIM)), 1)(got)


def solution(mesh):
    fine = Mesh(mesh.devices.reshape(2, ZHIGH, 2, -1), ("x", "zh", "zl", "head"))
    rows = ("x", "zh", "zl")
    return jax.shard_map(
        body,
        mesh=fine,
        in_specs=(P(rows, None), P(rows, None), P(rows, "head"), P(rows, "head")),
        out_specs=(P(rows, "head"), P(rows, "head")),
        check_vma=False,
    )
```

time: 1640 us -> 158 us (0.10)
  waiting for transfers between devices: 1520 us -> 25.1 us
  matrix products: 38.1 us -> 0 us
  starting transfers between devices: 0.47 us -> 24.5 us
  Pallas kernels: 0 us -> 23.5 us
  blocking collectives: 61.1 us -> 78.5 us
    psum x5 -> x0, waiting for transfers between devices: 1250 us -> none  [row_grams(): return lax.psum(values, 'dp')]
    reduce_scatter x2 -> x0, waiting for transfers between devices: 270 us -> none  [the longest x1 138 us: body(): lax.psum_scatter(latent_term(kv_latent, kv_cotangent), 'dp', scatter_dime...]
    psum x1 -> x0, blocking collectives: 61.1 us -> none  [row_norms(): return lax.psum(values, 'dp')]
    dot_general x32 -> x0, matrix products: 38.1 us -> none  [the longest x10 14.3 us: newton_schulz(): jnp.einsum('rhi,rhj->hij', matrix, matrix, precision=lax.Precision.HIGHEST)]
    unnamed x0 -> x1, blocking collectives: none -> 35.6 us
    all_gather x0 -> x1, blocking collectives: none -> 34.7 us  [body(): y = lax.all_gather(part[:USED], 'zh', axis=0, tiled=True)]
    ppermute x0 -> x6, waiting for transfers between devices: none -> 25.1 us  [the longest x1 10.4 us: body(): a_got = lax.ppermute(a_send, 'x', PAIR)]
    pallas_call x0 -> x5, Pallas kernels: none -> 23.5 us  [the longest x1 12.5 us: body(): call(update_kernel, shape(4, QOWN, LANES), 3, rows)(y, q_other, kv_other)]
  transfers between devices with their start and end apart: 7 -> 7, of which waited for: 7 -> 5; matrix products, arithmetic and copies ran while one was open for 0% -> 2% of each run, Pallas kernels for 0% -> 3%
where the time goes in v2:
time: 158 us; the launch traced here: 157 us
  blocking collectives  78.5 us (50%)
  waiting for transfers between devices  25.1 us (16%)
  starting transfers between devices  24.5 us (16%)
  Pallas kernels  23.5 us (15%)
  other arithmetic  2.13 us (1%)
  local copies, waits for them, and re-layouts  1.63 us (1%)
    unnamed x1, blocking collectives  35.6 us
    all_gather x1, blocking collectives, body(): y = lax.all_gather(part[:USED], 'zh', axis=0, tiled=True)  34.7 us
    pallas_call x1, Pallas kernels, body(): call(update_kernel, shape(4, QOWN, LANES), 3, rows)(y, q_other, kv_other)  12.5 us
    ppermute x1, waiting for transfers between devices, body(): a_got = lax.ppermute(a_send, 'x', PAIR)  10.4 us
    all_to_all x1, blocking collectives, body(): got = lax.all_to_all(ready, ('x', 'zl'), 0, 0)  8.15 us
    pallas_call x1, Pallas kernels, body(): call(keep_kernel, (half, half), 4, scratch, pltpu.HBM, cost, 60)(*args)  5.16 us
    pallas_call x1, Pallas kernels, body(): call(send_kernel, (half, half), 4, scratch, pltpu.HBM, cost, 60)(*args)  4.97 us
    ppermute x1, starting transfers between devices, body(): kv_other = lax.ppermute(y[QPART:], 'zl', [(0, 1)])  4.59 us
  transfers between devices with their start and end apart: 7, of which 5 were waited for; matrix products, arithmetic and copies ran while one was open for 2% of the time, Pallas kernels for 3%

profile of v2, /device:TPU:24, one launch (start us, length us, event | category | flops | bytes accessed | tf_op | source)
XLA Modules:
  0.0 156.8 jit_solution(12463166781837493057)
XLA Ops:
  0.6 5.0 %shard_map.60 = (f32[2,416,256]{2,1,0:T(8,128)}, f32[2,416,256]{2,1,0:T(8,128)}) custom-call(bf16[768,1536]{1,0:T(8,128)(2,1)} %ql.3, bf16[768,512]{1,0:T(8,128)(2,1)} %kl.3, bf16[768,384]{1,0:T(8,128)(2,1)} %qc.3, bf16[768,512]{1,0:T(8,128)(2,1)} %kc.3), custom_call_target="tpu_custom_call" | custom-call | flops 654311424 | bytes 8388608 | tf_op jit(solution)/shard_map/pallas_call | solution.py:234
  5.6 3.4 %collective-permute-start = (f32[2,416,256]{2,1,0:T(8,128)}, f32[2,416,256]{2,1,0:T(8,128)S(1)}, u32[]{:S(2)}, u32[]{:S(2)}) collective-permute-start(f32[2,416,256]{2,1,0:T(8,128)} %get-tuple-element.7), channel_id=1, source_target_pairs={{0,256},{256,0},{1,257},{257,1},{2,258},{258,2},{3,259},{259,3},{4... | collective-permute-start | bytes 2555912 | tf_op jit(solution)/shard_map/ppermute | solution.py:235
  9.0 3.8 %collective-permute-start.2 = (f32[2,416,256]{2,1,0:T(8,128)}, f32[2,416,256]{2,1,0:T(8,128)S(1)}, u32[]{:S(2)}, u32[]{:S(2)}) collective-permute-start(f32[2,416,256]{2,1,0:T(8,128)} %get-tuple-element.9), channel_id=1, source_target_pairs={{0,16},{16,0},{1,17},{17,1},{2,18},{18,2},{3,19},{19,3},{4,20},{20... | collective-permute-start | bytes 2555912 | tf_op jit(solution)/shard_map/ppermute | solution.py:236
  12.8 5.2 %shard_map.59 = (f32[2,416,256]{2,1,0:T(8,128)}, f32[2,416,256]{2,1,0:T(8,128)}) custom-call(bf16[768,1536]{1,0:T(8,128)(2,1)} %ql.3, bf16[768,512]{1,0:T(8,128)(2,1)} %kl.3, bf16[768,384]{1,0:T(8,128)(2,1)} %qc.3, bf16[768,512]{1,0:T(8,128)(2,1)} %kc.3), custom_call_target="tpu_custom_call" | custom-call | flops 654311424 | bytes 8388608 | tf_op jit(solution)/shard_map/pallas_call | solution.py:237
  18.0 0.0 copy-start
  18.0 0.0 copy-start.1
  18.0 10.4 %collective-permute-done.a_got = f32[2,416,256]{2,1,0:T(8,128)S(1)} collective-permute-done((f32[2,416,256]{2,1,0:T(8,128)}, f32[2,416,256]{2,1,0:T(8,128)S(1)}, u32[]{:S(2)}, u32[]{:S(2)}) %collective-permute-start) | collective-permute-done | bytes 852000 | tf_op jit(solution)/shard_map/ppermute | solution.py:235
  28.4 1.1 fusion.2
  29.5 3.8 %collective-permute-start.1 = (f32[416,256]{1,0:T(8,128)S(1)}, f32[416,256]{1,0:T(8,128)S(1)}, u32[]{:S(2)}, u32[]{:S(2)}) collective-permute-start(f32[416,256]{1,0:T(8,128)S(1)} %fusion.2), channel_id=1, source_target_pairs={{0,16},{16,0},{1,17},{17,1},{2,18},{18,2},{3,19},{19,3},{4,20},{20... | collective-permute-start | bytes 1277960 | tf_op jit(solution)/shard_map/ppermute | solution.py:238
  33.3 0.0 collective-permute-done.2.b_got
  33.3 1.1 fusion.1
  34.4 3.4 %collective-permute-start.3 = (f32[416,256]{1,0:T(8,128)S(1)}, f32[416,256]{1,0:T(8,128)S(1)}, u32[]{:S(2)}, u32[]{:S(2)}) collective-permute-start(f32[416,256]{1,0:T(8,128)S(1)} %fusion.1), channel_id=1, source_target_pairs={{0,256},{256,0},{1,257},{257,1},{2,258},{258,2},{3,259},{259,3},{4... | collective-permute-start | bytes 1277960 | tf_op jit(solution)/shard_map/ppermute | solution.py:239
  37.8 4.4 %collective-permute-done.1.a_next = f32[416,256]{1,0:T(8,128)S(1)} collective-permute-done((f32[416,256]{1,0:T(8,128)S(1)}, f32[416,256]{1,0:T(8,128)S(1)}, u32[]{:S(2)}, u32[]{:S(2)}) %collective-permute-start.1) | collective-permute-done | bytes 426016 | tf_op jit(solution)/shard_map/ppermute | solution.py:238
  42.2 4.4 %collective-permute-done.3.b_next = f32[416,256]{1,0:T(8,128)S(1)} collective-permute-done((f32[416,256]{1,0:T(8,128)S(1)}, f32[416,256]{1,0:T(8,128)S(1)}, u32[]{:S(2)}, u32[]{:S(2)}) %collective-permute-start.3) | collective-permute-done | bytes 426016 | tf_op jit(solution)/shard_map/ppermute | solution.py:239
  46.7 0.0 copy-done
  46.7 0.0 copy-done.1
  46.7 0.1 shard_map.61
  46.8 35.6 %fusion = f32[112,256]{1,0:T(8,128)S(1)} fusion(f32[888,256]{1,0:T(8,128)S(1)} %shard_map.61), kind=kCustom, calls=%all-reduce-scatter | all-reduce-scatter fusion | flops 229377 | bytes 1026048
  82.4 4.1 %collective-permute-start.6 = (f32[7,256]{1,0:T(8,128)S(1)}, f32[7,256]{1,0:T(8,128)S(1)}, u32[]{:S(2)}, u32[]{:S(2)}) collective-permute-start(f32[7,256]{1,0:T(8,128)S(1)} %slice.33), channel_id=1, source_target_pairs={{0,32},{32,64},{64,96},{96,128},{128,160},{160,192},{192,224},{1,3... | collective-permute-start | bytes 21512
  86.6 1.3 dynamic-slice.4
  88.5 0.0 collective-permute-done.6
  88.5 0.3 concatenate
  88.8 34.7 %all_gather.3.y = f32[832,256]{1,0:T(8,128)S(1)} all-gather(f32[104,256]{1,0:T(8,128)S(1)} %slice.30), channel_id=1, replica_groups=mesh['x'=2,'zh'=8,'zl'=2,'head'=16] {'zh'}, dimensions={0}, use_global_device_ids=true | all-gather | bytes 958464 | tf_op jit(solution)/shard_map/all_gather | solution.py:242
  123.6 1.3 collective-permute-start.4
  124.9 4.6 %collective-permute-start.5 = (f32[256,256]{1,0:T(8,128)S(1)}, f32[256,256]{1,0:T(8,128)S(1)}, u32[]{:S(2)}, u32[]{:S(2)}) collective-permute-start(f32[256,256]{1,0:T(8,128)S(1)} %slice.32), channel_id=1, source_target_pairs={{0,16},{1,17},{2,18},{3,19},{4,20},{5,21},{6,22},{7,23},{8,24},{9,... | collective-permute-start | bytes 786440 | tf_op jit(solution)/shard_map/ppermute | solution.py:244
  129.5 3.9 %collective-permute-done.5.kv_other = f32[256,256]{1,0:T(8,128)S(1)} collective-permute-done((f32[256,256]{1,0:T(8,128)S(1)}, f32[256,256]{1,0:T(8,128)S(1)}, u32[]{:S(2)}, u32[]{:S(2)}) %collective-permute-start.5) | collective-permute-done | bytes 262176 | tf_op jit(solution)/shard_map/ppermute | solution.py:244
  133.4 2.0 %collective-permute-done.4.q_other = f32[576,256]{1,0:T(8,128)S(1)} collective-permute-done((f32[576,256]{1,0:T(8,128)S(1)}, f32[576,256]{1,0:T(8,128)S(1)}, u32[]{:S(2)}, u32[]{:S(2)}) %collective-permute-start.4) | collective-permute-done | bytes 589856 | tf_op jit(solution)/shard_map/ppermute | solution.py:243
  135.4 12.5 %shard_map.62 = f32[4,48,256]{2,1,0:T(8,128)S(1)} custom-call(f32[832,256]{1,0:T(8,128)S(1)} %all_gather.3.y, f32[576,256]{1,0:T(8,128)S(1)} %collective-permute-done.4.q_other, f32[256,256]{1,0:T(8,128)S(1)} %collective-permute-done.5.kv_other), custom_call_target="tpu_custom_call" | custom-call | tf_op jit(solution)/shard_map/pallas_call | solution.py:246
  147.9 8.1 %all_to_all.5.got = f32[4,48,256]{2,1,0:T(8,128)S(1)} all-to-all(f32[4,48,256]{2,1,0:T(8,128)S(1)} %shard_map.62), channel_id=1, replica_groups=mesh['x'=2,'zh'=8,'zl'=2,'head'=16] {'x','zl'}, dimensions={0} | all-to-all | bytes 393216 | tf_op jit(solution)/shard_map/all_to_all | solution.py:247
  156.0 0.7 shard_map.63
  (5 shorter events, 0.1 us)
Async XLA Ops:
  5.6 22.8 %collective-permute-start = (f32[2,416,256]{2,1,0:T(8,128)}, f32[2,416,256]{2,1,0:T(8,128)S(1)}, u32[]{:S(2)}, u32[]{:S(2)}) collective-permute-start(f32[2,416,256]{2,1,0:T(8,128)} %get-tuple-element.7), channel_id=1, source_target_pairs={{0,256},{256,0},{1,257},{257,1},{2,258},{258,2},{3,259},{259,3},{4... | collective-permute-start | bytes 2555912 | tf_op jit(solution)/shard_map/ppermute | solution.py:235
  9.0 24.3 %collective-permute-start.2 = (f32[2,416,256]{2,1,0:T(8,128)}, f32[2,416,256]{2,1,0:T(8,128)S(1)}, u32[]{:S(2)}, u32[]{:S(2)}) collective-permute-start(f32[2,416,256]{2,1,0:T(8,128)} %get-tuple-element.9), channel_id=1, source_target_pairs={{0,16},{16,0},{1,17},{17,1},{2,18},{18,2},{3,19},{19,3},{4,20},{20... | collective-permute-start | bytes 2555912 | tf_op jit(solution)/shard_map/ppermute | solution.py:236
  18.0 28.7 %copy-start = (f32[2,416,256]{2,1,0:T(8,128)S(1)}, f32[2,416,256]{2,1,0:T(8,128)}, u32[]{:S(2)}) copy-start(f32[2,416,256]{2,1,0:T(8,128)} %get-tuple-element.6.a_keep) | copy-start | bytes 2555908
  18.0 28.7 %copy-start.1 = (f32[2,416,256]{2,1,0:T(8,128)S(1)}, f32[2,416,256]{2,1,0:T(8,128)}, u32[]{:S(2)}) copy-start(f32[2,416,256]{2,1,0:T(8,128)} %get-tuple-element.8.b_keep) | copy-start | bytes 2555908
  29.5 12.8 %collective-permute-start.1 = (f32[416,256]{1,0:T(8,128)S(1)}, f32[416,256]{1,0:T(8,128)S(1)}, u32[]{:S(2)}, u32[]{:S(2)}) collective-permute-start(f32[416,256]{1,0:T(8,128)S(1)} %fusion.2), channel_id=1, source_target_pairs={{0,16},{16,0},{1,17},{17,1},{2,18},{18,2},{3,19},{19,3},{4,20},{20... | collective-permute-start | bytes 1277960 | tf_op jit(solution)/shard_map/ppermute | solution.py:238
  34.4 12.3 %collective-permute-start.3 = (f32[416,256]{1,0:T(8,128)S(1)}, f32[416,256]{1,0:T(8,128)S(1)}, u32[]{:S(2)}, u32[]{:S(2)}) collective-permute-start(f32[416,256]{1,0:T(8,128)S(1)} %fusion.1), channel_id=1, source_target_pairs={{0,256},{256,0},{1,257},{257,1},{2,258},{258,2},{3,259},{259,3},{4... | collective-permute-start | bytes 1277960 | tf_op jit(solution)/shard_map/ppermute | solution.py:239
  82.4 6.1 %collective-permute-start.6 = (f32[7,256]{1,0:T(8,128)S(1)}, f32[7,256]{1,0:T(8,128)S(1)}, u32[]{:S(2)}, u32[]{:S(2)}) collective-permute-start(f32[7,256]{1,0:T(8,128)S(1)} %slice.33), channel_id=1, source_target_pairs={{0,32},{32,64},{64,96},{96,128},{128,160},{160,192},{192,224},{1,3... | collective-permute-start | bytes 21512
  123.6 11.8 %collective-permute-start.4 = (f32[576,256]{1,0:T(8,128)S(1)}, f32[576,256]{1,0:T(8,128)S(1)}, u32[]{:S(2)}, u32[]{:S(2)}) collective-permute-start(f32[576,256]{1,0:T(8,128)S(1)} %slice.31), channel_id=1, source_target_pairs={{16,0},{17,1},{18,2},{19,3},{20,4},{21,5},{22,6},{23,7},{24,8},{25... | collective-permute-start | bytes 1769480 | tf_op jit(solution)/shard_map/ppermute | solution.py:243
  124.9 8.5 %collective-permute-start.5 = (f32[256,256]{1,0:T(8,128)S(1)}, f32[256,256]{1,0:T(8,128)S(1)}, u32[]{:S(2)}, u32[]{:S(2)}) collective-permute-start(f32[256,256]{1,0:T(8,128)S(1)} %slice.32), channel_id=1, source_target_pairs={{0,16},{1,17},{2,18},{3,19},{4,20},{5,21},{6,22},{7,23},{8,24},{9,... | collective-permute-start | bytes 786440 | tf_op jit(solution)/shard_map/ppermute | solution.py:244

commit v3 on v2

v3 whole, which is shorter than its diff:
```python
import math

import jax
import jax.numpy as jnp
from jax import lax
from jax.experimental import pallas as pl
from jax.experimental.pallas import tpu as pltpu
from jax.sharding import Mesh, PartitionSpec as P

QRANK = 1536
KVRANK = 512
QDIM = 192
KVDIM = 256
ITERS = 5
RESTART = 3

COEF_A = 3.4445
COEF_B = -4.775
COEF_C = 2.0315
EPSILON = 1e-06

LANES = 256
QTILES = QRANK // LANES
KVTILES = KVRANK // LANES
HEAD_ROWS = QTILES * QDIM + KVTILES * KVDIM
PART = HEAD_ROWS // 2
CUT = PART // 2
QHERE = PART // QDIM
QREST = PART - QHERE * QDIM
QMORE = QTILES * QDIM - PART
ZHIGH = 8
USED = PART // ZHIGH
SHARD = USED + 7
QOWN = QRANK // 32
KVOWN = KVRANK // 32
MEBI = 1024 * 1024
VMEM = pl.BlockSpec(memory_space=pltpu.VMEM)
F32 = jnp.float32


def dot(lhs, rhs, dims):
    return lax.dot_general(
        lhs, rhs, (dims, ((), ())), precision=lax.Precision.HIGHEST, preferred_element_type=F32
    )


def mul(lhs, rhs):
    return dot(lhs, rhs, ((1,), (0,)))


def products(cot, start, stop, lat):
    return lax.dot_general(
        cot[:, start:stop], lat, (((0,), (0,)), ((), ())), preferred_element_type=F32
    )


def fill(part, low, high, q_cot, kv_cot, ql, kl, out):
    base = part * PART
    at = base + low
    while at < base + high:
        in_q = at < QTILES * QDIM
        width, first, cot, lat = (QDIM, 0, q_cot, ql) if in_q else (KVDIM, QTILES * QDIM, kv_cot, kl)
        tile, start = divmod(at - first, width)
        stop = min(width, start + base + high - at)
        block = products(cot, start, stop, lat[:, tile * LANES : (tile + 1) * LANES])
        out[at - base - low : at - base - low + stop - start, :] = block
        at += stop - start


def heads(qc, kc, x, away):
    second = (x ^ away) == 1
    q_cot = jnp.where(second, qc[:, QDIM:], qc[:, :QDIM])
    return q_cot, jnp.where(second, kc[:, KVDIM:], kc[:, :KVDIM])


def send_kernel(ql, kl, qc, kc, a_send, b_send, ql_v, kl_v, qc_v, kc_v, sems):
    x, z = lax.axis_index("x"), lax.axis_index("zl")
    pairs = ((qc, qc_v), (kc, kc_v), (ql, ql_v), (kl, kl_v))
    copies = [pltpu.make_async_copy(src, dst, sems.at[k]) for k, (src, dst) in enumerate(pairs)]
    for copy in copies:
        copy.start()
    for copy in copies:
        copy.wait()
    q_cot, kv_cot = heads(qc_v, kc_v, x, 1)
    for part in range(2):
        fill(part, 0, CUT, q_cot, kv_cot, ql_v, kl_v, a_send.at[z ^ part])
    for part in range(2):

        @pl.when(z != part)
        def _(part=part):
            for away in range(2):
                q_cot, kv_cot = heads(qc_v, kc_v, x, away)
                fill(part, CUT, PART, q_cot, kv_cot, ql_v, kl_v, b_send.at[away])


def keep_kernel(ql, kl, qc, kc, a_keep, b_keep, ql_v, kl_v, qc_v, kc_v, sems):
    x, z = lax.axis_index("x"), lax.axis_index("zl")
    pairs = ((qc, qc_v), (kc, kc_v), (ql, ql_v), (kl, kl_v))
    copies = [pltpu.make_async_copy(src, dst, sems.at[k]) for k, (src, dst) in enumerate(pairs)]
    for copy in copies:
        copy.start()
    for copy in copies:
        copy.wait()
    q_cot, kv_cot = heads(qc_v, kc_v, x, 0)
    for part in range(2):
        fill(part, 0, CUT, q_cot, kv_cot, ql_v, kl_v, a_keep.at[z ^ part])
    for part in range(2):

        @pl.when(z == part)
        def _(part=part):
            for away in range(2):
                q_cot, kv_cot = heads(qc_v, kc_v, x, away)
                fill(part, CUT, PART, q_cot, kv_cot, ql_v, kl_v, b_keep.at[away])


def place_kernel(a_keep, a_got, a_next, b_keep, b_got, b_next, out):
    for index in range(ZHIGH):
        for keep, got, last, low in ((a_keep, a_got, a_next, 0), (b_keep, b_got, b_next, CUT)):
            start, stop = max(index * USED, low), min((index + 1) * USED, low + CUT)
            if start < stop:
                rows = slice(start - low, stop - low)
                where = index * SHARD + start - index * USED
                out[where : where + stop - start, :] = keep[0, rows, :] + got[0, rows, :] + last[rows, :]
        out[index * SHARD + USED : (index + 1) * SHARD, :] = jnp.zeros((SHARD - USED, LANES), F32)


def identity(size):
    rows = lax.broadcasted_iota(jnp.int32, (size, size), 0)
    return rows == lax.broadcasted_iota(jnp.int32, (size, size), 1)


def steps(gram, count):
    product = None
    for index in range(count):
        poly = COEF_B * gram + COEF_C * mul(gram, gram)
        if product is None:
            product = jnp.where(identity(poly.shape[0]), COEF_A + poly, poly)
        else:
            product = COEF_A * product + mul(product, poly)
        if index + 1 < count:
            inner = COEF_A * gram + mul(gram, poly)
            gram = COEF_A * inner + mul(poly, inner)
    return product


def gram_of(wide):
    def term(lhs, rhs):
        return lax.dot_general(lhs, rhs, (((1,), (1,)), ((), ())), preferred_element_type=F32)

    high = wide.astype(jnp.bfloat16)
    rest = wide - high.astype(F32)
    mid = rest.astype(jnp.bfloat16)
    low = (rest - mid.astype(F32)).astype(jnp.bfloat16)
    cross = term(high, mid) + (term(high, low) + 0.5 * term(mid, mid))
    return term(high, high) + (cross + cross.T)


def orthogonalize(tiles, norm, rows):
    wide = jnp.concatenate(tiles, axis=1)
    gram = gram_of(wide)
    trace = jnp.sum(jnp.where(identity(gram.shape[0]), gram, 0.0))
    scale = lax.rsqrt(jnp.full((1, 1), trace + EPSILON, F32))
    product = steps(gram * scale * scale, RESTART)
    wide = mul(product * scale, wide)
    product = steps(gram_of(wide), ITERS - RESTART)
    rows[...] = dot(wide, product * norm, ((0,), (0,)))


def update_kernel(y, other, out, q_rows, kv_rows):
    z, high = lax.axis_index("zl"), lax.axis_index("zh")

    @pl.when(z == 0)
    def _():
        tiles = [y[t * QDIM : (t + 1) * QDIM, :] for t in range(QHERE)]
        tiles.append(jnp.concatenate((y[QHERE * QDIM :, :], other[: QDIM - QREST, :]), axis=0))
        tiles += [other[t * QDIM - PART : (t + 1) * QDIM - PART, :] for t in range(QHERE + 1, QTILES)]
        orthogonalize(tiles, math.sqrt(QRANK), q_rows)
        for half in range(2):
            for k in range(2):
                start = pl.multiple_of(half * (QRANK // 2) + (2 * high + k) * QOWN, 8)
                out[2 * half + k, :, :QDIM] = q_rows[pl.ds(start, QOWN), :]
                out[2 * half + k, :, QDIM:] = jnp.zeros((QOWN, LANES - QDIM), F32)

    @pl.when(z == 1)
    def _():
        tiles = [y[QMORE + t * KVDIM : QMORE + (t + 1) * KVDIM, :] for t in range(KVTILES)]
        orthogonalize(tiles, math.sqrt(KVRANK), kv_rows)
        for half in range(2):
            for k in range(2):
                start = pl.multiple_of(half * (KVRANK // 2) + (2 * high + k) * KVOWN, 8)
                out[2 * half + k, :KVOWN, :] = kv_rows[pl.ds(start, KVOWN), :]
                out[2 * half + k, KVOWN:, :] = jnp.zeros((QOWN - KVOWN, LANES), F32)


def join_kernel(got, q_out, kv_out):
    for head in range(2):
        q_out[:, head * QDIM : (head + 1) * QDIM] = got[2 * head, :, :QDIM]
        kv_out[:, head * KVDIM : (head + 1) * KVDIM] = got[2 * head + 1, :KVOWN, :]


def shape(*dims):
    return jax.ShapeDtypeStruct(dims, F32)


def call(kernel, outs, inputs, scratch=(), space=pltpu.VMEM, cost=None, vmem=24):
    single = not isinstance(outs, tuple)
    return pl.pallas_call(
        kernel,
        out_shape=outs,
        in_specs=[pl.BlockSpec(memory_space=space)] * inputs,
        out_specs=VMEM if single else (VMEM,) * len(outs),
        scratch_shapes=list(scratch),
        compiler_params=pltpu.CompilerParams(vmem_limit_bytes=vmem * MEBI),
        cost_estimate=cost,
    )


PAIR = [(0, 1), (1, 0)]


def body(q_latent, kv_latent, q_cotangent, kv_cotangent):
    half = shape(2, CUT, LANES)
    tokens = q_latent.shape[0]
    args = (q_latent, kv_latent, q_cotangent, kv_cotangent)
    scratch = [pltpu.VMEM(arg.shape, arg.dtype) for arg in args] + [pltpu.SemaphoreType.DMA((4,))]
    cost = pl.CostEstimate(flops=2 * tokens * 2 * 2 * CUT * LANES, bytes_accessed=8 << 20, transcendentals=0)
    a_send, b_send = call(send_kernel, (half, half), 4, scratch, pltpu.HBM, cost, 60)(*args)
    a_got = lax.ppermute(a_send, "x", PAIR)
    b_got = lax.ppermute(b_send, "zl", PAIR)
    a_keep, b_keep = call(keep_kernel, (half, half), 4, scratch, pltpu.HBM, cost, 24)(*args)
    a_next = lax.ppermute(a_keep[1] + a_got[1], "zl", PAIR)
    b_next = lax.ppermute(b_keep[1] + b_got[1], "x", PAIR)
    placed = call(place_kernel, shape(ZHIGH * SHARD, LANES), 6)(a_keep, a_got, a_next, b_keep, b_got, b_next)
    part = lax.optimization_barrier(lax.psum_scatter(placed, "zh", scatter_dimension=0, tiled=True))
    y = lax.all_gather(part[:USED], "zh", axis=0, tiled=True)
    other = lax.ppermute(y[:QMORE], "zl", [(1, 0)])
    rows = (pltpu.VMEM((QRANK, QDIM), F32), pltpu.VMEM((KVRANK, KVDIM), F32))
    ready = call(update_kernel, shape(4, QOWN, LANES), 2, rows)(y, other)
    got = lax.all_to_all(ready, ("x", "zl"), 0, 0)
    return call(join_kernel, (shape(QOWN, 2 * QDIM), shape(KVOWN, 2 * KVDIM)), 1)(got)


def solution(mesh):
    fine = Mesh(mesh.devices.reshape(2, ZHIGH, 2, -1), ("x", "zh", "zl", "head"))
    rows = ("x", "zh", "zl")
    return jax.shard_map(
        body,
        mesh=fine,
        in_specs=(P(rows, None), P(rows, None), P(rows, "head"), P(rows, "head")),
        out_specs=(P(rows, "head"), P(rows, "head")),
        check_vma=False,
    )
```

time: 158 us -> 152 us (0.962)
  starting transfers between devices: 24.5 us -> 20.2 us
  Pallas kernels: 23.5 us -> 19.5 us
  waiting for transfers between devices: 25.1 us -> 27.3 us
  other arithmetic: 2.13 us -> 0.11 us
  blocking collectives: 78.5 us -> 80.1 us
    ppermute x2 -> x1, starting transfers between devices: 5.89 us -> 1.29 us  [body(): other = lax.ppermute(y[:QMORE], 'zl', [(1, 0)])]
    pallas_call x2, Pallas kernels: 17.7 us -> 13.1 us  [the longest x1 10 us: body(): ready = call(update_kernel, shape(4, QOWN, LANES), 2, rows)(y, other)]
    ppermute x2 -> x1, waiting for transfers between devices: 5.85 us -> 7.67 us  [body(): other = lax.ppermute(y[:QMORE], 'zl', [(1, 0)])]
  transfers between devices with their start and end apart: 7 -> 6, of which waited for: 5 -> 4; matrix products, arithmetic and copies ran while one was open for 2% -> 1% of each run, Pallas kernels for 3% -> 2%
where the time goes in v3:
time: 152 us; the launch traced here: 151 us
  blocking collectives  80.1 us (53%)
  waiting for transfers between devices  27.3 us (18%)
  starting transfers between devices  20.2 us (13%)
  Pallas kernels  19.5 us (13%)
  local copies, waits for them, and re-layouts  2.66 us (2%)
    all_gather x1, blocking collectives, body(): y = lax.all_gather(part[:USED], 'zh', axis=0, tiled=True)  36.1 us
    unnamed x1, blocking collectives  36.1 us
    ppermute x1, waiting for transfers between devices, body(): a_got = lax.ppermute(a_send, 'x', PAIR)  10.7 us
    pallas_call x1, Pallas kernels, body(): ready = call(update_kernel, shape(4, QOWN, LANES), 2, rows)(y, other)  10 us
    all_to_all x1, blocking collectives, body(): got = lax.all_to_all(ready, ('x', 'zl'), 0, 0)  7.92 us
    ppermute x1, waiting for transfers between devices, body(): other = lax.ppermute(y[:QMORE], 'zl', [(1, 0)])  7.67 us
    pallas_call x1, Pallas kernels, body(): call(send_kernel, (half, half), 4, scratch, pltpu.HBM, cost, 60)(*args)  5.61 us
    ppermute x1, waiting for transfers between devices, body(): a_next = lax.ppermute(a_keep[1] + a_got[1], 'zl', PAIR)  5.45 us
  transfers between devices with their start and end apart: 6, of which 4 were waited for; matrix products, arithmetic and copies ran while one was open for 1% of the time, Pallas kernels for 2%

profile of v3, /device:TPU:24, one launch (start us, length us, event | category | flops | bytes accessed | tf_op | source)
XLA Modules:
  0.0 151.4 jit_solution(1121454604229789672)
XLA Ops:
  0.6 0.0 copy-start
  0.6 0.0 copy-start.1
  0.6 0.0 copy-start.2
  0.7 5.6 %shard_map.60 = (f32[2,416,256]{2,1,0:T(8,128)}, f32[2,416,256]{2,1,0:T(8,128)}) custom-call(bf16[768,1536]{1,0:T(8,128)(2,1)} %ql.3, bf16[768,512]{1,0:T(8,128)(2,1)} %kl.3, bf16[768,384]{1,0:T(8,128)(2,1)} %qc.3, bf16[768,512]{1,0:T(8,128)(2,1)} %kc.3), custom_call_target="tpu_custom_call" | custom-call | flops 654311424 | bytes 8388608 | tf_op jit(solution)/shard_map/pallas_call | solution.py:227
  6.3 3.4 %collective-permute-start = (f32[2,416,256]{2,1,0:T(8,128)}, f32[2,416,256]{2,1,0:T(8,128)S(1)}, u32[]{:S(2)}, u32[]{:S(2)}) collective-permute-start(f32[2,416,256]{2,1,0:T(8,128)} %get-tuple-element.7), channel_id=1, source_target_pairs={{0,256},{256,0},{1,257},{257,1},{2,258},{258,2},{3,259},{259,3},{4... | collective-permute-start | bytes 2555912 | tf_op jit(solution)/shard_map/ppermute | solution.py:228
  9.7 4.5 %collective-permute-start.2 = (f32[2,416,256]{2,1,0:T(8,128)}, f32[2,416,256]{2,1,0:T(8,128)S(1)}, u32[]{:S(2)}, u32[]{:S(2)}) collective-permute-start(f32[2,416,256]{2,1,0:T(8,128)} %get-tuple-element.9), channel_id=1, source_target_pairs={{0,16},{16,0},{1,17},{17,1},{2,18},{18,2},{3,19},{19,3},{4,20},{20... | collective-permute-start | bytes 2555912 | tf_op jit(solution)/shard_map/ppermute | solution.py:229
  14.2 0.0 copy-done
  14.2 0.0 copy-done.1
  14.2 0.0 copy-done.2
  14.2 0.0 copy-start.3
  14.3 1.1 copy-done.3
  15.3 3.1 %shard_map.59 = (f32[2,416,256]{2,1,0:T(8,128)S(1)}, f32[2,416,256]{2,1,0:T(8,128)S(1)}) custom-call(bf16[768,1536]{1,0:T(8,128)(2,1)S(1)} %copy-done, bf16[768,512]{1,0:T(8,128)(2,1)S(1)} %copy-done.1, bf16[768,384]{1,0:T(8,128)(2,1)S(1)} %copy-done.3, bf16[768,512]{1,0:T(8,128)(2,1)S(1)} %copy-done.2), custom_call_target="tpu_custom_call" | custom-call | flops 654311424 | bytes 8388608 | tf_op jit(solution)/shard_map/pallas_call | solution.py:230
  18.4 10.7 %collective-permute-done.a_got = f32[2,416,256]{2,1,0:T(8,128)S(1)} collective-permute-done((f32[2,416,256]{2,1,0:T(8,128)}, f32[2,416,256]{2,1,0:T(8,128)S(1)}, u32[]{:S(2)}, u32[]{:S(2)}) %collective-permute-start) | collective-permute-done | bytes 852000 | tf_op jit(solution)/shard_map/ppermute | solution.py:228
  29.1 0.1 fusion.2
  29.1 4.5 %collective-permute-start.1 = (f32[416,256]{1,0:T(8,128)S(1)}, f32[416,256]{1,0:T(8,128)S(1)}, u32[]{:S(2)}, u32[]{:S(2)}) collective-permute-start(f32[416,256]{1,0:T(8,128)S(1)} %fusion.2), channel_id=1, source_target_pairs={{0,16},{16,0},{1,17},{17,1},{2,18},{18,2},{3,19},{19,3},{4,20},{20... | collective-permute-start | bytes 1277960 | tf_op jit(solution)/shard_map/ppermute | solution.py:231
  33.6 0.0 collective-permute-done.2.b_got
  33.7 0.1 fusion.1
  33.7 3.4 %collective-permute-start.3 = (f32[416,256]{1,0:T(8,128)S(1)}, f32[416,256]{1,0:T(8,128)S(1)}, u32[]{:S(2)}, u32[]{:S(2)}) collective-permute-start(f32[416,256]{1,0:T(8,128)S(1)} %fusion.1), channel_id=1, source_target_pairs={{0,256},{256,0},{1,257},{257,1},{2,258},{258,2},{3,259},{259,3},{4... | collective-permute-start | bytes 1277960 | tf_op jit(solution)/shard_map/ppermute | solution.py:232
  37.1 5.4 %collective-permute-done.1.a_next = f32[416,256]{1,0:T(8,128)S(1)} collective-permute-done((f32[416,256]{1,0:T(8,128)S(1)}, f32[416,256]{1,0:T(8,128)S(1)}, u32[]{:S(2)}, u32[]{:S(2)}) %collective-permute-start.1) | collective-permute-done | bytes 426016 | tf_op jit(solution)/shard_map/ppermute | solution.py:231
  42.6 3.4 %collective-permute-done.3.b_next = f32[416,256]{1,0:T(8,128)S(1)} collective-permute-done((f32[416,256]{1,0:T(8,128)S(1)}, f32[416,256]{1,0:T(8,128)S(1)}, u32[]{:S(2)}, u32[]{:S(2)}) %collective-permute-start.3) | collective-permute-done | bytes 426016 | tf_op jit(solution)/shard_map/ppermute | solution.py:232
  46.0 0.1 shard_map.61
  46.1 36.1 %fusion = f32[112,256]{1,0:T(8,128)S(1)} fusion(f32[888,256]{1,0:T(8,128)S(1)} %shard_map.61), kind=kCustom, calls=%all-reduce-scatter | all-reduce-scatter fusion | flops 229377 | bytes 1026048
  82.2 3.1 %collective-permute-start.5 = (f32[7,256]{1,0:T(8,128)S(1)}, f32[7,256]{1,0:T(8,128)S(1)}, u32[]{:S(2)}, u32[]{:S(2)}) collective-permute-start(f32[7,256]{1,0:T(8,128)S(1)} %slice.28), channel_id=1, source_target_pairs={{0,32},{32,64},{64,96},{96,128},{128,160},{160,192},{192,224},{1,3... | collective-permute-start | bytes 21512
  85.3 1.3 dynamic-slice.4
  87.2 0.0 collective-permute-done.5
  87.2 0.3 concatenate
  87.6 36.1 %all_gather.3.y = f32[832,256]{1,0:T(8,128)S(1)} all-gather(f32[104,256]{1,0:T(8,128)S(1)} %slice.26), channel_id=1, replica_groups=mesh['x'=2,'zh'=8,'zl'=2,'head'=16] {'zh'}, dimensions={0}, use_global_device_ids=true | all-gather | bytes 958464 | tf_op jit(solution)/shard_map/all_gather | solution.py:235
  123.7 1.3 collective-permute-start.4
  125.0 7.7 %collective-permute-done.4.other = f32[320,256]{1,0:T(8,128)S(1)} collective-permute-done((f32[320,256]{1,0:T(8,128)S(1)}, f32[320,256]{1,0:T(8,128)S(1)}, u32[]{:S(2)}, u32[]{:S(2)}) %collective-permute-start.4) | collective-permute-done | bytes 327712 | tf_op jit(solution)/shard_map/ppermute | solution.py:236
  132.7 10.0 %shard_map.62 = f32[4,48,256]{2,1,0:T(8,128)S(1)} custom-call(f32[832,256]{1,0:T(8,128)S(1)} %all_gather.3.y, f32[320,256]{1,0:T(8,128)S(1)} %collective-permute-done.4.other), custom_call_target="tpu_custom_call" | custom-call | tf_op jit(solution)/shard_map/pallas_call | solution.py:238
  142.7 7.9 %all_to_all.5.got = f32[4,48,256]{2,1,0:T(8,128)S(1)} all-to-all(f32[4,48,256]{2,1,0:T(8,128)S(1)} %shard_map.62), channel_id=1, replica_groups=mesh['x'=2,'zh'=8,'zl'=2,'head'=16] {'x','zl'}, dimensions={0} | all-to-all | bytes 393216 | tf_op jit(solution)/shard_map/all_to_all | solution.py:239
  150.6 0.7 shard_map.63
  (4 shorter events, 0.1 us)
Async XLA Ops:
  0.6 13.6 %copy-start = (bf16[768,1536]{1,0:T(8,128)(2,1)S(1)}, bf16[768,1536]{1,0:T(8,128)(2,1)}, u32[]{:S(2)}) copy-start(bf16[768,1536]{1,0:T(8,128)(2,1)} %ql.3) | copy-start | bytes 7077892
  0.6 13.6 %copy-start.1 = (bf16[768,512]{1,0:T(8,128)(2,1)S(1)}, bf16[768,512]{1,0:T(8,128)(2,1)}, u32[]{:S(2)}) copy-start(bf16[768,512]{1,0:T(8,128)(2,1)} %kl.3) | copy-start | bytes 2359300
  0.6 13.6 %copy-start.2 = (bf16[768,512]{1,0:T(8,128)(2,1)S(1)}, bf16[768,512]{1,0:T(8,128)(2,1)}, u32[]{:S(2)}) copy-start(bf16[768,512]{1,0:T(8,128)(2,1)} %kc.3) | copy-start | bytes 2359300
  6.3 22.8 %collective-permute-start = (f32[2,416,256]{2,1,0:T(8,128)}, f32[2,416,256]{2,1,0:T(8,128)S(1)}, u32[]{:S(2)}, u32[]{:S(2)}) collective-permute-start(f32[2,416,256]{2,1,0:T(8,128)} %get-tuple-element.7), channel_id=1, source_target_pairs={{0,256},{256,0},{1,257},{257,1},{2,258},{258,2},{3,259},{259,3},{4... | collective-permute-start | bytes 2555912 | tf_op jit(solution)/shard_map/ppermute | solution.py:228
  9.7 24.0 %collective-permute-start.2 = (f32[2,416,256]{2,1,0:T(8,128)}, f32[2,416,256]{2,1,0:T(8,128)S(1)}, u32[]{:S(2)}, u32[]{:S(2)}) collective-permute-start(f32[2,416,256]{2,1,0:T(8,128)} %get-tuple-element.9), channel_id=1, source_target_pairs={{0,16},{16,0},{1,17},{17,1},{2,18},{18,2},{3,19},{19,3},{4,20},{20... | collective-permute-start | bytes 2555912 | tf_op jit(solution)/shard_map/ppermute | solution.py:229
  14.2 1.1 copy-start.3
  29.1 13.4 %collective-permute-start.1 = (f32[416,256]{1,0:T(8,128)S(1)}, f32[416,256]{1,0:T(8,128)S(1)}, u32[]{:S(2)}, u32[]{:S(2)}) collective-permute-start(f32[416,256]{1,0:T(8,128)S(1)} %fusion.2), channel_id=1, source_target_pairs={{0,16},{16,0},{1,17},{17,1},{2,18},{18,2},{3,19},{19,3},{4,20},{20... | collective-permute-start | bytes 1277960 | tf_op jit(solution)/shard_map/ppermute | solution.py:231
  33.7 12.3 %collective-permute-start.3 = (f32[416,256]{1,0:T(8,128)S(1)}, f32[416,256]{1,0:T(8,128)S(1)}, u32[]{:S(2)}, u32[]{:S(2)}) collective-permute-start(f32[416,256]{1,0:T(8,128)S(1)} %fusion.1), channel_id=1, source_target_pairs={{0,256},{256,0},{1,257},{257,1},{2,258},{258,2},{3,259},{259,3},{4... | collective-permute-start | bytes 1277960 | tf_op jit(solution)/shard_map/ppermute | solution.py:232
  82.2 5.0 %collective-permute-start.5 = (f32[7,256]{1,0:T(8,128)S(1)}, f32[7,256]{1,0:T(8,128)S(1)}, u32[]{:S(2)}, u32[]{:S(2)}) collective-permute-start(f32[7,256]{1,0:T(8,128)S(1)} %slice.28), channel_id=1, source_target_pairs={{0,32},{32,64},{64,96},{96,128},{128,160},{160,192},{192,224},{1,3... | collective-permute-start | bytes 21512
  123.7 9.0 %collective-permute-start.4 = (f32[320,256]{1,0:T(8,128)S(1)}, f32[320,256]{1,0:T(8,128)S(1)}, u32[]{:S(2)}, u32[]{:S(2)}) collective-permute-start(f32[320,256]{1,0:T(8,128)S(1)} %slice.27), channel_id=1, source_target_pairs={{16,0},{17,1},{18,2},{19,3},{20,4},{21,5},{22,6},{23,7},{24,8},{25... | collective-permute-start | bytes 983048 | tf_op jit(solution)/shard_map/ppermute | solution.py:236

commit v4 on v3

--- a/solution.py
+++ b/solution.py
@@ -28,9 +28,8 @@
 QHERE = PART // QDIM
 QREST = PART - QHERE * QDIM
 QMORE = QTILES * QDIM - PART
-ZHIGH = 8
-USED = PART // ZHIGH
-SHARD = USED + 7
+PIECE = 8
+PIECES = PART // PIECE
 QOWN = QRANK // 32
 KVOWN = KVRANK // 32
 MEBI = 1024 * 1024
@@ -113,15 +112,12 @@
                 fill(part, CUT, PART, q_cot, kv_cot, ql_v, kl_v, b_keep.at[away])
 
 
-def place_kernel(a_keep, a_got, a_next, b_keep, b_got, b_next, out):
-    for index in range(ZHIGH):
-        for keep, got, last, low in ((a_keep, a_got, a_next, 0), (b_keep, b_got, b_next, CUT)):
-            start, stop = max(index * USED, low), min((index + 1) * USED, low + CUT)
-            if start < stop:
-                rows = slice(start - low, stop - low)
-                where = index * SHARD + start - index * USED
-                out[where : where + stop - start, :] = keep[0, rows, :] + got[0, rows, :] + last[rows, :]
-        out[index * SHARD + USED : (index + 1) * SHARD, :] = jnp.zeros((SHARD - USED, LANES), F32)
+def add_kernel(a_keep, a_got, a_next, b_keep, b_got, b_next, *outs):
+    for k, out in enumerate(outs):
+        low = k * PIECE
+        keep, got, last = (a_keep, a_got, a_next) if low < CUT else (b_keep, b_got, b_next)
+        rows = slice(low % CUT, low % CUT + PIECE)
+        out[...] = keep[0, rows, :] + got[0, rows, :] + last[rows, :]
 
 
 def identity(size):
@@ -166,13 +162,18 @@
     rows[...] = dot(wide, product * norm, ((0,), (0,)))
 
 
-def update_kernel(y, other, out, q_rows, kv_rows):
+def update_kernel(*refs):
+    pieces, (other, out, q_rows, kv_rows) = refs[:PIECES], refs[PIECES:]
+
+    def y(low, high):
+        return jnp.concatenate([ref[...] for ref in pieces[low // PIECE : high // PIECE]], axis=0)
+
     z, high = lax.axis_index("zl"), lax.axis_index("zh")
 
     @pl.when(z == 0)
     def _():
-        tiles = [y[t * QDIM : (t + 1) * QDIM, :] for t in range(QHERE)]
-        tiles.append(jnp.concatenate((y[QHERE * QDIM :, :], other[: QDIM - QREST, :]), axis=0))
+        tiles = [y(t * QDIM, (t + 1) * QDIM) for t in range(QHERE)]
+        tiles.append(jnp.concatenate((y(QHERE * QDIM, PART), other[: QDIM - QREST, :]), axis=0))
         tiles += [other[t * QDIM - PART : (t + 1) * QDIM - PART, :] for t in range(QHERE + 1, QTILES)]
         orthogonalize(tiles, math.sqrt(QRANK), q_rows)
         for half in range(2):
@@ -183,7 +184,7 @@
 
     @pl.when(z == 1)
     def _():
-        tiles = [y[QMORE + t * KVDIM : QMORE + (t + 1) * KVDIM, :] for t in range(KVTILES)]
+        tiles = [y(QMORE + t * KVDIM, QMORE + (t + 1) * KVDIM) for t in range(KVTILES)]
         orthogonalize(tiles, math.sqrt(KVRANK), kv_rows)
         for half in range(2):
             for k in range(2):
@@ -230,18 +231,19 @@
     a_keep, b_keep = call(keep_kernel, (half, half), 4, scratch, pltpu.HBM, cost, 24)(*args)
     a_next = lax.ppermute(a_keep[1] + a_got[1], "zl", PAIR)
     b_next = lax.ppermute(b_keep[1] + b_got[1], "x", PAIR)
-    placed = call(place_kernel, shape(ZHIGH * SHARD, LANES), 6)(a_keep, a_got, a_next, b_keep, b_got, b_next)
-    part = lax.optimization_barrier(lax.psum_scatter(placed, "zh", scatter_dimension=0, tiled=True))
-    y = lax.all_gather(part[:USED], "zh", axis=0, tiled=True)
-    other = lax.ppermute(y[:QMORE], "zl", [(1, 0)])
+    parts = (a_keep, a_got, a_next, b_keep, b_got, b_next)
+    pieces = call(add_kernel, (shape(PIECE, LANES),) * PIECES, 6)(*parts)
+    sums = lax.psum(tuple(pieces), "zh")
+    leaving = jnp.concatenate(sums[: QMORE // PIECE], axis=0)
+    other = lax.ppermute(leaving, "zl", [(1, 0)])
     rows = (pltpu.VMEM((QRANK, QDIM), F32), pltpu.VMEM((KVRANK, KVDIM), F32))
-    ready = call(update_kernel, shape(4, QOWN, LANES), 2, rows)(y, other)
+    ready = call(update_kernel, shape(4, QOWN, LANES), PIECES + 1, rows)(*sums, other)
     got = lax.all_to_all(ready, ("x", "zl"), 0, 0)
     return call(join_kernel, (shape(QOWN, 2 * QDIM), shape(KVOWN, 2 * KVDIM)), 1)(got)
 
 
 def solution(mesh):
-    fine = Mesh(mesh.devices.reshape(2, ZHIGH, 2, -1), ("x", "zh", "zl", "head"))
+    fine = Mesh(mesh.devices.reshape(2, 8, 2, -1), ("x", "zh", "zl", "head"))
     rows = ("x", "zh", "zl")
     return jax.shard_map(
         body,

time: 152 us -> 138 us (0.908)
  blocking collectives: 80.1 us -> 70.3 us
  starting transfers between devices: 20.2 us -> 16.3 us
    psum x0 -> x1, blocking collectives: none -> 62.4 us  [body(): sums = lax.psum(tuple(pieces), 'zh')]
    all_gather x1 -> x0, blocking collectives: 36.1 us -> none  [body(): y = lax.all_gather(part[:USED], 'zh', axis=0, tiled=True)]
    unnamed x1 -> x0, blocking collectives: 36.1 us -> none
    ppermute x1, waiting for transfers between devices: 0.01 us -> 11.6 us  [body(): b_got = lax.ppermute(b_send, 'zl', PAIR)]
    ppermute x1, waiting for transfers between devices: 10.7 us -> 0.01 us  [body(): a_got = lax.ppermute(a_send, 'x', PAIR)]
    unnamed x1 -> x0, starting transfers between devices: 3.07 us -> none
    ppermute x1, waiting for transfers between devices: 3.44 us -> 5.77 us  [body(): b_next = lax.ppermute(b_keep[1] + b_got[1], 'x', PAIR)]
    ppermute x1, waiting for transfers between devices: 5.45 us -> 3.18 us  [body(): a_next = lax.ppermute(a_keep[1] + a_got[1], 'zl', PAIR)]
  transfers between devices with their start and end apart: 6 -> 5, of which waited for: 4 -> 4; matrix products, arithmetic and copies ran while one was open for 1% -> 0% of each run, Pallas kernels for 2% -> 2%
where the time goes in v4:
time: 138 us; the launch traced here: 137 us
  blocking collectives  70.3 us (51%)
  waiting for transfers between devices  28.2 us (20%)
  Pallas kernels  19.6 us (14%)
  starting transfers between devices  16.3 us (12%)
    psum x1, blocking collectives, body(): sums = lax.psum(tuple(pieces), 'zh')  62.4 us
    ppermute x1, waiting for transfers between devices, body(): b_got = lax.ppermute(b_send, 'zl', PAIR)  11.6 us
    pallas_call x1, Pallas kernels, body(): call(update_kernel, shape(4, QOWN, LANES), PIECES + 1, rows)(*sums, other)  10.1 us
    all_to_all x1, blocking collectives, body(): got = lax.all_to_all(ready, ('x', 'zl'), 0, 0)  7.92 us
    ppermute x1, waiting for transfers between devices, body(): other = lax.ppermute(leaving, 'zl', [(1, 0)])  7.67 us
    ppermute x1, waiting for transfers between devices, body(): b_next = lax.ppermute(b_keep[1] + b_got[1], 'x', PAIR)  5.77 us
    pallas_call x1, Pallas kernels, body(): call(send_kernel, (half, half), 4, scratch, pltpu.HBM, cost, 60)(*args)  5.61 us
    ppermute x1, starting transfers between devices, body(): b_got = lax.ppermute(b_send, 'zl', PAIR)  4.51 us
  transfers between devices with their start and end apart: 5, of which 4 were waited for; matrix products, arithmetic and copies ran while one was open for 0% of the time, Pallas kernels for 2%

profile of v4, /device:TPU:24, one launch (start us, length us, event | category | flops | bytes accessed | tf_op | source)
XLA Modules:
  0.0 136.7 jit_solution(4445690146094790671)
XLA Ops:
  0.6 0.0 copy-start.2
  0.6 0.0 copy-start.1
  0.6 0.0 copy-start
  0.7 5.6 %shard_map.60 = (f32[2,416,256]{2,1,0:T(8,128)}, f32[2,416,256]{2,1,0:T(8,128)}) custom-call(bf16[768,1536]{1,0:T(8,128)(2,1)} %ql.3, bf16[768,512]{1,0:T(8,128)(2,1)} %kl.3, bf16[768,384]{1,0:T(8,128)(2,1)} %qc.3, bf16[768,512]{1,0:T(8,128)(2,1)} %kc.3), custom_call_target="tpu_custom_call" | custom-call | flops 654311424 | bytes 8388608 | tf_op jit(solution)/shard_map/pallas_call | solution.py:228
  6.3 4.5 %collective-permute-start.2 = (f32[2,416,256]{2,1,0:T(8,128)}, f32[2,416,256]{2,1,0:T(8,128)S(1)}, u32[]{:S(2)}, u32[]{:S(2)}) collective-permute-start(f32[2,416,256]{2,1,0:T(8,128)} %get-tuple-element.113), channel_id=1, source_target_pairs={{0,16},{16,0},{1,17},{17,1},{2,18},{18,2},{3,19},{19,3},{4,20},{20... | collective-permute-start | bytes 2555912 | tf_op jit(solution)/shard_map/ppermute | solution.py:230
  10.8 3.4 %collective-permute-start = (f32[2,416,256]{2,1,0:T(8,128)}, f32[2,416,256]{2,1,0:T(8,128)S(1)}, u32[]{:S(2)}, u32[]{:S(2)}) collective-permute-start(f32[2,416,256]{2,1,0:T(8,128)} %get-tuple-element.111), channel_id=1, source_target_pairs={{0,256},{256,0},{1,257},{257,1},{2,258},{258,2},{3,259},{259,3},{4... | collective-permute-start | bytes 2555912 | tf_op jit(solution)/shard_map/ppermute | solution.py:229
  14.2 0.0 copy-done.2
  14.2 0.0 copy-done.1
  14.2 0.0 copy-done
  14.2 0.0 copy-start.3
  14.3 1.1 copy-done.3
  15.3 3.1 %shard_map.59 = (f32[2,416,256]{2,1,0:T(8,128)S(1)}, f32[2,416,256]{2,1,0:T(8,128)S(1)}) custom-call(bf16[768,1536]{1,0:T(8,128)(2,1)S(1)} %copy-done, bf16[768,512]{1,0:T(8,128)(2,1)S(1)} %copy-done.1, bf16[768,384]{1,0:T(8,128)(2,1)S(1)} %copy-done.3, bf16[768,512]{1,0:T(8,128)(2,1)S(1)} %copy-done.2), custom_call_target="tpu_custom_call" | custom-call | flops 654311424 | bytes 8388608 | tf_op jit(solution)/shard_map/pallas_call | solution.py:231
  18.4 11.6 %collective-permute-done.2.b_got = f32[2,416,256]{2,1,0:T(8,128)S(1)} collective-permute-done((f32[2,416,256]{2,1,0:T(8,128)}, f32[2,416,256]{2,1,0:T(8,128)S(1)}, u32[]{:S(2)}, u32[]{:S(2)}) %collective-permute-start.2) | collective-permute-done | bytes 852000 | tf_op jit(solution)/shard_map/ppermute | solution.py:230
  29.9 0.1 fusion
  30.0 3.4 %collective-permute-start.3 = (f32[416,256]{1,0:T(8,128)S(1)}, f32[416,256]{1,0:T(8,128)S(1)}, u32[]{:S(2)}, u32[]{:S(2)}) collective-permute-start(f32[416,256]{1,0:T(8,128)S(1)} %fusion), channel_id=1, source_target_pairs={{0,256},{256,0},{1,257},{257,1},{2,258},{258,2},{3,259},{259,3},{4... | collective-permute-start | bytes 1277960 | tf_op jit(solution)/shard_map/ppermute | solution.py:233
  33.4 0.0 collective-permute-done.a_got
  33.4 0.1 fusion.1
  33.5 3.6 %collective-permute-start.1 = (f32[416,256]{1,0:T(8,128)S(1)}, f32[416,256]{1,0:T(8,128)S(1)}, u32[]{:S(2)}, u32[]{:S(2)}) collective-permute-start(f32[416,256]{1,0:T(8,128)S(1)} %fusion.1), channel_id=1, source_target_pairs={{0,16},{16,0},{1,17},{17,1},{2,18},{18,2},{3,19},{19,3},{4,20},{20... | collective-permute-start | bytes 1277960 | tf_op jit(solution)/shard_map/ppermute | solution.py:232
  37.1 5.8 %collective-permute-done.3.b_next = f32[416,256]{1,0:T(8,128)S(1)} collective-permute-done((f32[416,256]{1,0:T(8,128)S(1)}, f32[416,256]{1,0:T(8,128)S(1)}, u32[]{:S(2)}, u32[]{:S(2)}) %collective-permute-start.3) | collective-permute-done | bytes 426016 | tf_op jit(solution)/shard_map/ppermute | solution.py:233
  42.9 3.2 %collective-permute-done.1.a_next = f32[416,256]{1,0:T(8,128)S(1)} collective-permute-done((f32[416,256]{1,0:T(8,128)S(1)}, f32[416,256]{1,0:T(8,128)S(1)}, u32[]{:S(2)}, u32[]{:S(2)}) %collective-permute-start.1) | collective-permute-done | bytes 426016 | tf_op jit(solution)/shard_map/ppermute | solution.py:232
  46.1 0.1 shard_map.61
  46.2 62.4 %all-reduce.2 = (f32[8,256]{1,0:T(8,128)S(1)}, f32[8,256]{1,0:T(8,128)S(1)}, f32[8,256]{1,0:T(8,128)S(1)}, f32[8,256]{1,0:T(8,128)S(1)}, f32[8,256]{1,0:T(8,128)...) all-reduce(f32[8,256]{1,0:T(8,128)S(1)} %get-tuple-element.114, ...), channel_id=1, replica_groups=mesh['x'=2,'zh'=8,'zl'=2,'head'=16] {'zh'}, use_global_device_ids=true, to_apply=%region_0.0 | all-reduce | flops 212992 | bytes 1703936 | tf_op jit(solution)/shard_map/psum | solution.py:236
  109.0 1.3 collective-permute-start.4
  110.3 7.7 %collective-permute-done.4.refs_104_ = f32[320,256]{1,0:T(8,128)S(1)} collective-permute-done((f32[320,256]{1,0:T(8,128)S(1)}, f32[320,256]{1,0:T(8,128)S(1)}, u32[]{:S(2)}, u32[]{:S(2)}) %collective-permute-start.4) | collective-permute-done | bytes 327712 | tf_op jit(solution)/shard_map/ppermute | solution.py:238
  118.0 10.1 %shard_map.62 = f32[4,48,256]{2,1,0:T(8,128)S(1)} custom-call(f32[8,256]{1,0:T(8,128)S(1)} %get-tuple-element.218.refs_0_, f32[8,256]{1,0:T(8,128)S(1)} %get-tuple-element.219.refs_1_, f32[8,256]{1,0:T(8,128)S(1)} %get-tuple-element.220.refs_2_, f32[8,256]{1,0:T(8,128)S(1)} %get-tuple-element.221.refs_3_, f32[8,256]{1,0:T(8,128)S(1)} %get-tuple-element.222.refs_4_, ...), custom_call_target="tpu_custom_call" | custom-call | tf_op jit(solution)/shard_map/pallas_call | solution.py:240
  128.1 7.9 %all_to_all.5.got = f32[4,48,256]{2,1,0:T(8,128)S(1)} all-to-all(f32[4,48,256]{2,1,0:T(8,128)S(1)} %shard_map.62), channel_id=1, replica_groups=mesh['x'=2,'zh'=8,'zl'=2,'head'=16] {'x','zl'}, dimensions={0} | all-to-all | bytes 393216 | tf_op jit(solution)/shard_map/all_to_all | solution.py:241
  136.0 0.7 shard_map.63
  (40 shorter events, 0.1 us)
Async XLA Ops:
  0.6 13.6 %copy-start.2 = (bf16[768,512]{1,0:T(8,128)(2,1)S(1)}, bf16[768,512]{1,0:T(8,128)(2,1)}, u32[]{:S(2)}) copy-start(bf16[768,512]{1,0:T(8,128)(2,1)} %kc.3) | copy-start | bytes 2359300
  0.6 13.6 %copy-start.1 = (bf16[768,512]{1,0:T(8,128)(2,1)S(1)}, bf16[768,512]{1,0:T(8,128)(2,1)}, u32[]{:S(2)}) copy-start(bf16[768,512]{1,0:T(8,128)(2,1)} %kl.3) | copy-start | bytes 2359300
  0.6 13.6 %copy-start = (bf16[768,1536]{1,0:T(8,128)(2,1)S(1)}, bf16[768,1536]{1,0:T(8,128)(2,1)}, u32[]{:S(2)}) copy-start(bf16[768,1536]{1,0:T(8,128)(2,1)} %ql.3) | copy-start | bytes 7077892
  6.3 23.7 %collective-permute-start.2 = (f32[2,416,256]{2,1,0:T(8,128)}, f32[2,416,256]{2,1,0:T(8,128)S(1)}, u32[]{:S(2)}, u32[]{:S(2)}) collective-permute-start(f32[2,416,256]{2,1,0:T(8,128)} %get-tuple-element.113), channel_id=1, source_target_pairs={{0,16},{16,0},{1,17},{17,1},{2,18},{18,2},{3,19},{19,3},{4,20},{20... | collective-permute-start | bytes 2555912 | tf_op jit(solution)/shard_map/ppermute | solution.py:230
  10.8 22.6 %collective-permute-start = (f32[2,416,256]{2,1,0:T(8,128)}, f32[2,416,256]{2,1,0:T(8,128)S(1)}, u32[]{:S(2)}, u32[]{:S(2)}) collective-permute-start(f32[2,416,256]{2,1,0:T(8,128)} %get-tuple-element.111), channel_id=1, source_target_pairs={{0,256},{256,0},{1,257},{257,1},{2,258},{258,2},{3,259},{259,3},{4... | collective-permute-start | bytes 2555912 | tf_op jit(solution)/shard_map/ppermute | solution.py:229
  14.2 1.1 copy-start.3
  30.0 12.9 %collective-permute-start.3 = (f32[416,256]{1,0:T(8,128)S(1)}, f32[416,256]{1,0:T(8,128)S(1)}, u32[]{:S(2)}, u32[]{:S(2)}) collective-permute-start(f32[416,256]{1,0:T(8,128)S(1)} %fusion), channel_id=1, source_target_pairs={{0,256},{256,0},{1,257},{257,1},{2,258},{258,2},{3,259},{259,3},{4... | collective-permute-start | bytes 1277960 | tf_op jit(solution)/shard_map/ppermute | solution.py:233
  33.5 12.6 %collective-permute-start.1 = (f32[416,256]{1,0:T(8,128)S(1)}, f32[416,256]{1,0:T(8,128)S(1)}, u32[]{:S(2)}, u32[]{:S(2)}) collective-permute-start(f32[416,256]{1,0:T(8,128)S(1)} %fusion.1), channel_id=1, source_target_pairs={{0,16},{16,0},{1,17},{17,1},{2,18},{18,2},{3,19},{19,3},{4,20},{20... | collective-permute-start | bytes 1277960 | tf_op jit(solution)/shard_map/ppermute | solution.py:232
  109.0 9.0 %collective-permute-start.4 = (f32[320,256]{1,0:T(8,128)S(1)}, f32[320,256]{1,0:T(8,128)S(1)}, u32[]{:S(2)}, u32[]{:S(2)}) collective-permute-start(f32[320,256]{1,0:T(8,128)S(1)} %constant_dynamic-update-slice_fusion), channel_id=1, source_target_pairs={{16,0},{17,1},{18,2},{19,3},{20,4},{21,5},{22,6},{23,7},{24,8},{25... | collective-permute-start | bytes 983048 | tf_op jit(solution)/shard_map/ppermute | solution.py:238

commit v5 on v4

--- a/solution.py
+++ b/solution.py
@@ -28,8 +28,9 @@
 QHERE = PART // QDIM
 QREST = PART - QHERE * QDIM
 QMORE = QTILES * QDIM - PART
-PIECE = 8
-PIECES = PART // PIECE
+SIZES = (16,) * 38 + (8,) * 28
+STARTS = tuple(sum(SIZES[:k]) for k in range(len(SIZES)))
+PIECES = len(SIZES)
 QOWN = QRANK // 32
 KVOWN = KVRANK // 32
 MEBI = 1024 * 1024
@@ -74,15 +75,18 @@
 
 def send_kernel(ql, kl, qc, kc, a_send, b_send, ql_v, kl_v, qc_v, kc_v, sems):
     x, z = lax.axis_index("x"), lax.axis_index("zl")
-    pairs = ((qc, qc_v), (kc, kc_v), (ql, ql_v), (kl, kl_v))
+    pairs = ((qc, qc_v), (ql, ql_v), (kc, kc_v), (kl, kl_v))
     copies = [pltpu.make_async_copy(src, dst, sems.at[k]) for k, (src, dst) in enumerate(pairs)]
     for copy in copies:
         copy.start()
-    for copy in copies:
-        copy.wait()
+    copies[0].wait()
+    copies[1].wait()
+    q_cot = jnp.where(x == 0, qc_v[:, QDIM:], qc_v[:, :QDIM])
+    fill(0, 0, CUT, q_cot, None, ql_v, None, a_send.at[z])
+    copies[2].wait()
+    copies[3].wait()
     q_cot, kv_cot = heads(qc_v, kc_v, x, 1)
-    for part in range(2):
-        fill(part, 0, CUT, q_cot, kv_cot, ql_v, kl_v, a_send.at[z ^ part])
+    fill(1, 0, CUT, q_cot, kv_cot, ql_v, kl_v, a_send.at[z ^ 1])
     for part in range(2):
 
         @pl.when(z != part)
@@ -114,9 +118,9 @@
 
 def add_kernel(a_keep, a_got, a_next, b_keep, b_got, b_next, *outs):
     for k, out in enumerate(outs):
-        low = k * PIECE
+        low = STARTS[k]
         keep, got, last = (a_keep, a_got, a_next) if low < CUT else (b_keep, b_got, b_next)
-        rows = slice(low % CUT, low % CUT + PIECE)
+        rows = slice(low % CUT, low % CUT + SIZES[k])
         out[...] = keep[0, rows, :] + got[0, rows, :] + last[rows, :]
 
 
@@ -166,7 +170,7 @@
     pieces, (other, out, q_rows, kv_rows) = refs[:PIECES], refs[PIECES:]
 
     def y(low, high):
-        return jnp.concatenate([ref[...] for ref in pieces[low // PIECE : high // PIECE]], axis=0)
+        return jnp.concatenate([ref[...] for ref, at in zip(pieces, STARTS) if low <= at < high], axis=0)
 
     z, high = lax.axis_index("zl"), lax.axis_index("zh")
 
@@ -232,9 +236,9 @@
     a_next = lax.ppermute(a_keep[1] + a_got[1], "zl", PAIR)
     b_next = lax.ppermute(b_keep[1] + b_got[1], "x", PAIR)
     parts = (a_keep, a_got, a_next, b_keep, b_got, b_next)
-    pieces = call(add_kernel, (shape(PIECE, LANES),) * PIECES, 6)(*parts)
+    pieces = call(add_kernel, tuple(shape(size, LANES) for size in SIZES), 6)(*parts)
     sums = lax.psum(tuple(pieces), "zh")
-    leaving = jnp.concatenate(sums[: QMORE // PIECE], axis=0)
+    leaving = jnp.concatenate(sums[: STARTS.index(QMORE)], axis=0)
     other = lax.ppermute(leaving, "zl", [(1, 0)])
     rows = (pltpu.VMEM((QRANK, QDIM), F32), pltpu.VMEM((KVRANK, KVDIM), F32))
     ready = call(update_kernel, shape(4, QOWN, LANES), PIECES + 1, rows)(*sums, other)

time: 138 us -> 137 us (level)
  no operation moved by 1% of the time
where the time goes in v5:
time: 137 us; the launch traced here: 136 us
  blocking collectives  69.3 us (51%)
  waiting for transfers between devices  29 us (21%)
  Pallas kernels  19.6 us (14%)
  starting transfers between devices  16.2 us (12%)
    psum x1, blocking collectives, body(): sums = lax.psum(tuple(pieces), 'zh')  61.4 us
    ppermute x1, waiting for transfers between devices, body(): b_got = lax.ppermute(b_send, 'zl', PAIR)  11.6 us
    pallas_call x1, Pallas kernels, body(): call(update_kernel, shape(4, QOWN, LANES), PIECES + 1, rows)(*sums, other)  10 us
    ppermute x1, waiting for transfers between devices, body(): other = lax.ppermute(leaving, 'zl', [(1, 0)])  8.51 us
    all_to_all x1, blocking collectives, body(): got = lax.all_to_all(ready, ('x', 'zl'), 0, 0)  7.92 us
    ppermute x1, waiting for transfers between devices, body(): b_next = lax.ppermute(b_keep[1] + b_got[1], 'x', PAIR)  5.77 us
    pallas_call x1, Pallas kernels, body(): call(send_kernel, (half, half), 4, scratch, pltpu.HBM, cost, 60)(*args)  5.72 us
    ppermute x1, starting transfers between devices, body(): b_got = lax.ppermute(b_send, 'zl', PAIR)  4.51 us
  transfers between devices with their start and end apart: 5, of which 4 were waited for; matrix products, arithmetic and copies ran while one was open for 0% of the time, Pallas kernels for 2%

profile of v5, /device:TPU:24, one launch (start us, length us, event | category | flops | bytes accessed | tf_op | source)
XLA Modules:
  0.0 136.5 jit_solution(11776844730293670793)
XLA Ops:
  0.6 0.0 copy-start.2
  0.6 0.0 copy-start.1
  0.6 0.0 copy-start
  0.7 5.7 %shard_map.60 = (f32[2,416,256]{2,1,0:T(8,128)}, f32[2,416,256]{2,1,0:T(8,128)}) custom-call(bf16[768,1536]{1,0:T(8,128)(2,1)} %ql.3, bf16[768,512]{1,0:T(8,128)(2,1)} %kl.3, bf16[768,384]{1,0:T(8,128)(2,1)} %qc.3, bf16[768,512]{1,0:T(8,128)(2,1)} %kc.3), custom_call_target="tpu_custom_call" | custom-call | flops 654311424 | bytes 8388608 | tf_op jit(solution)/shard_map/pallas_call | solution.py:232
  6.4 4.5 %collective-permute-start.2 = (f32[2,416,256]{2,1,0:T(8,128)}, f32[2,416,256]{2,1,0:T(8,128)S(1)}, u32[]{:S(2)}, u32[]{:S(2)}) collective-permute-start(f32[2,416,256]{2,1,0:T(8,128)} %get-tuple-element.75), channel_id=1, source_target_pairs={{0,16},{16,0},{1,17},{17,1},{2,18},{18,2},{3,19},{19,3},{4,20},{20... | collective-permute-start | bytes 2555912 | tf_op jit(solution)/shard_map/ppermute | solution.py:234
  10.9 3.4 %collective-permute-start = (f32[2,416,256]{2,1,0:T(8,128)}, f32[2,416,256]{2,1,0:T(8,128)S(1)}, u32[]{:S(2)}, u32[]{:S(2)}) collective-permute-start(f32[2,416,256]{2,1,0:T(8,128)} %get-tuple-element.73), channel_id=1, source_target_pairs={{0,256},{256,0},{1,257},{257,1},{2,258},{258,2},{3,259},{259,3},{4... | collective-permute-start | bytes 2555912 | tf_op jit(solution)/shard_map/ppermute | solution.py:233
  14.3 0.0 copy-done.2
  14.3 0.0 copy-done.1
  14.3 0.0 copy-done
  14.3 0.0 copy-start.3
  14.3 1.1 copy-done.3
  15.4 3.1 %shard_map.59 = (f32[2,416,256]{2,1,0:T(8,128)S(1)}, f32[2,416,256]{2,1,0:T(8,128)S(1)}) custom-call(bf16[768,1536]{1,0:T(8,128)(2,1)S(1)} %copy-done, bf16[768,512]{1,0:T(8,128)(2,1)S(1)} %copy-done.1, bf16[768,384]{1,0:T(8,128)(2,1)S(1)} %copy-done.3, bf16[768,512]{1,0:T(8,128)(2,1)S(1)} %copy-done.2), custom_call_target="tpu_custom_call" | custom-call | flops 654311424 | bytes 8388608 | tf_op jit(solution)/shard_map/pallas_call | solution.py:235
  18.5 11.6 %collective-permute-done.2.b_got = f32[2,416,256]{2,1,0:T(8,128)S(1)} collective-permute-done((f32[2,416,256]{2,1,0:T(8,128)}, f32[2,416,256]{2,1,0:T(8,128)S(1)}, u32[]{:S(2)}, u32[]{:S(2)}) %collective-permute-start.2) | collective-permute-done | bytes 852000 | tf_op jit(solution)/shard_map/ppermute | solution.py:234
  30.0 0.1 fusion
  30.1 3.4 %collective-permute-start.3 = (f32[416,256]{1,0:T(8,128)S(1)}, f32[416,256]{1,0:T(8,128)S(1)}, u32[]{:S(2)}, u32[]{:S(2)}) collective-permute-start(f32[416,256]{1,0:T(8,128)S(1)} %fusion), channel_id=1, source_target_pairs={{0,256},{256,0},{1,257},{257,1},{2,258},{258,2},{3,259},{259,3},{4... | collective-permute-start | bytes 1277960 | tf_op jit(solution)/shard_map/ppermute | solution.py:237
  33.5 0.0 collective-permute-done.a_got
  33.5 0.1 fusion.1
  33.6 3.6 %collective-permute-start.1 = (f32[416,256]{1,0:T(8,128)S(1)}, f32[416,256]{1,0:T(8,128)S(1)}, u32[]{:S(2)}, u32[]{:S(2)}) collective-permute-start(f32[416,256]{1,0:T(8,128)S(1)} %fusion.1), channel_id=1, source_target_pairs={{0,16},{16,0},{1,17},{17,1},{2,18},{18,2},{3,19},{19,3},{4,20},{20... | collective-permute-start | bytes 1277960 | tf_op jit(solution)/shard_map/ppermute | solution.py:236
  37.2 5.8 %collective-permute-done.3.b_next = f32[416,256]{1,0:T(8,128)S(1)} collective-permute-done((f32[416,256]{1,0:T(8,128)S(1)}, f32[416,256]{1,0:T(8,128)S(1)}, u32[]{:S(2)}, u32[]{:S(2)}) %collective-permute-start.3) | collective-permute-done | bytes 426016 | tf_op jit(solution)/shard_map/ppermute | solution.py:237
  43.0 3.2 %collective-permute-done.1.a_next = f32[416,256]{1,0:T(8,128)S(1)} collective-permute-done((f32[416,256]{1,0:T(8,128)S(1)}, f32[416,256]{1,0:T(8,128)S(1)}, u32[]{:S(2)}, u32[]{:S(2)}) %collective-permute-start.1) | collective-permute-done | bytes 426016 | tf_op jit(solution)/shard_map/ppermute | solution.py:236
  46.2 0.1 shard_map.61
  46.3 61.4 %all-reduce.2 = (f32[16,256]{1,0:T(8,128)S(1)}, f32[16,256]{1,0:T(8,128)S(1)}, f32[16,256]{1,0:T(8,128)S(1)}, f32[16,256]{1,0:T(8,128)S(1)}, f32[16,256]{1,0:T(8...) all-reduce(f32[16,256]{1,0:T(8,128)S(1)} %get-tuple-element.76, ...), channel_id=1, replica_groups=mesh['x'=2,'zh'=8,'zl'=2,'head'=16] {'zh'}, use_global_device_ids=true, to_apply=%region_0.0 | all-reduce | flops 212992 | bytes 1703936 | tf_op jit(solution)/shard_map/psum | solution.py:240
  108.0 1.3 collective-permute-start.4
  109.3 8.5 %collective-permute-done.4.refs_66_ = f32[320,256]{1,0:T(8,128)S(1)} collective-permute-done((f32[320,256]{1,0:T(8,128)S(1)}, f32[320,256]{1,0:T(8,128)S(1)}, u32[]{:S(2)}, u32[]{:S(2)}) %collective-permute-start.4) | collective-permute-done | bytes 327712 | tf_op jit(solution)/shard_map/ppermute | solution.py:242
  117.8 10.0 %shard_map.62 = f32[4,48,256]{2,1,0:T(8,128)S(1)} custom-call(f32[16,256]{1,0:T(8,128)S(1)} %get-tuple-element.142.refs_0_, f32[16,256]{1,0:T(8,128)S(1)} %get-tuple-element.143.refs_1_, f32[16,256]{1,0:T(8,128)S(1)} %get-tuple-element.144.refs_2_, f32[16,256]{1,0:T(8,128)S(1)} %get-tuple-element.145.refs_3_, f32[16,256]{1,0:T(8,128)S(1)} %get-tuple-element.146.refs_4_, ...), custom_call_target="tpu_custom_call" | custom-call | tf_op jit(solution)/shard_map/pallas_call | solution.py:244
  127.8 7.9 %all_to_all.5.got = f32[4,48,256]{2,1,0:T(8,128)S(1)} all-to-all(f32[4,48,256]{2,1,0:T(8,128)S(1)} %shard_map.62), channel_id=1, replica_groups=mesh['x'=2,'zh'=8,'zl'=2,'head'=16] {'x','zl'}, dimensions={0} | all-to-all | bytes 393216 | tf_op jit(solution)/shard_map/all_to_all | solution.py:245
  135.7 0.7 shard_map.63
  (20 shorter events, 0.1 us)
Async XLA Ops:
  0.6 13.7 %copy-start.2 = (bf16[768,512]{1,0:T(8,128)(2,1)S(1)}, bf16[768,512]{1,0:T(8,128)(2,1)}, u32[]{:S(2)}) copy-start(bf16[768,512]{1,0:T(8,128)(2,1)} %kc.3) | copy-start | bytes 2359300
  0.6 13.7 %copy-start.1 = (bf16[768,512]{1,0:T(8,128)(2,1)S(1)}, bf16[768,512]{1,0:T(8,128)(2,1)}, u32[]{:S(2)}) copy-start(bf16[768,512]{1,0:T(8,128)(2,1)} %kl.3) | copy-start | bytes 2359300
  0.6 13.7 %copy-start = (bf16[768,1536]{1,0:T(8,128)(2,1)S(1)}, bf16[768,1536]{1,0:T(8,128)(2,1)}, u32[]{:S(2)}) copy-start(bf16[768,1536]{1,0:T(8,128)(2,1)} %ql.3) | copy-start | bytes 7077892
  6.4 23.7 %collective-permute-start.2 = (f32[2,416,256]{2,1,0:T(8,128)}, f32[2,416,256]{2,1,0:T(8,128)S(1)}, u32[]{:S(2)}, u32[]{:S(2)}) collective-permute-start(f32[2,416,256]{2,1,0:T(8,128)} %get-tuple-element.75), channel_id=1, source_target_pairs={{0,16},{16,0},{1,17},{17,1},{2,18},{18,2},{3,19},{19,3},{4,20},{20... | collective-permute-start | bytes 2555912 | tf_op jit(solution)/shard_map/ppermute | solution.py:234
  10.9 22.6 %collective-permute-start = (f32[2,416,256]{2,1,0:T(8,128)}, f32[2,416,256]{2,1,0:T(8,128)S(1)}, u32[]{:S(2)}, u32[]{:S(2)}) collective-permute-start(f32[2,416,256]{2,1,0:T(8,128)} %get-tuple-element.73), channel_id=1, source_target_pairs={{0,256},{256,0},{1,257},{257,1},{2,258},{258,2},{3,259},{259,3},{4... | collective-permute-start | bytes 2555912 | tf_op jit(solution)/shard_map/ppermute | solution.py:233
  14.3 1.1 copy-start.3
  30.1 12.9 %collective-permute-start.3 = (f32[416,256]{1,0:T(8,128)S(1)}, f32[416,256]{1,0:T(8,128)S(1)}, u32[]{:S(2)}, u32[]{:S(2)}) collective-permute-start(f32[416,256]{1,0:T(8,128)S(1)} %fusion), channel_id=1, source_target_pairs={{0,256},{256,0},{1,257},{257,1},{2,258},{258,2},{3,259},{259,3},{4... | collective-permute-start | bytes 1277960 | tf_op jit(solution)/shard_map/ppermute | solution.py:237
  33.6 12.6 %collective-permute-start.1 = (f32[416,256]{1,0:T(8,128)S(1)}, f32[416,256]{1,0:T(8,128)S(1)}, u32[]{:S(2)}, u32[]{:S(2)}) collective-permute-start(f32[416,256]{1,0:T(8,128)S(1)} %fusion.1), channel_id=1, source_target_pairs={{0,16},{16,0},{1,17},{17,1},{2,18},{18,2},{3,19},{19,3},{4,20},{20... | collective-permute-start | bytes 1277960 | tf_op jit(solution)/shard_map/ppermute | solution.py:236
  108.0 9.8 %collective-permute-start.4 = (f32[320,256]{1,0:T(8,128)S(1)}, f32[320,256]{1,0:T(8,128)S(1)}, u32[]{:S(2)}, u32[]{:S(2)}) collective-permute-start(f32[320,256]{1,0:T(8,128)S(1)} %constant_dynamic-update-slice_fusion), channel_id=1, source_target_pairs={{16,0},{17,1},{18,2},{19,3},{20,4},{21,5},{22,6},{23,7},{24,8},{25... | collective-permute-start | bytes 983048 | tf_op jit(solution)/shard_map/ppermute | solution.py:242

commit v6 on v5

--- a/solution.py
+++ b/solution.py
@@ -33,6 +33,8 @@
 PIECES = len(SIZES)
 QOWN = QRANK // 32
 KVOWN = KVRANK // 32
+QSPAN = 256
+KVSPAN = 128
 MEBI = 1024 * 1024
 VMEM = pl.BlockSpec(memory_space=pltpu.VMEM)
 F32 = jnp.float32
@@ -155,7 +157,7 @@
     return term(high, high) + (cross + cross.T)
 
 
-def orthogonalize(tiles, norm, rows):
+def orthogonalize(tiles, norm, own, span, wide_v, rows):
     wide = jnp.concatenate(tiles, axis=1)
     gram = gram_of(wide)
     trace = jnp.sum(jnp.where(identity(gram.shape[0]), gram, 0.0))
@@ -163,11 +165,17 @@
     product = steps(gram * scale * scale, RESTART)
     wide = mul(product * scale, wide)
     product = steps(gram_of(wide), ITERS - RESTART)
-    rows[...] = dot(wide, product * norm, ((0,), (0,)))
+    wide_v[...] = wide
+    half_lanes = wide.shape[1] // 2
+    first = jnp.minimum((own // 128) * 128, half_lanes - span)
+    for half in range(2):
+        lanes = pl.ds(pl.multiple_of(half * half_lanes + first, 128), span)
+        rows[half] = dot(wide_v[:, lanes], product * norm, ((0,), (0,)))
+    return own - first
 
 
 def update_kernel(*refs):
-    pieces, (other, out, q_rows, kv_rows) = refs[:PIECES], refs[PIECES:]
+    pieces, (other, out, q_wide, kv_wide, q_rows, kv_rows) = refs[:PIECES], refs[PIECES:]
 
     def y(low, high):
         return jnp.concatenate([ref[...] for ref, at in zip(pieces, STARTS) if low <= at < high], axis=0)
@@ -179,21 +187,21 @@
         tiles = [y(t * QDIM, (t + 1) * QDIM) for t in range(QHERE)]
         tiles.append(jnp.concatenate((y(QHERE * QDIM, PART), other[: QDIM - QREST, :]), axis=0))
         tiles += [other[t * QDIM - PART : (t + 1) * QDIM - PART, :] for t in range(QHERE + 1, QTILES)]
-        orthogonalize(tiles, math.sqrt(QRANK), q_rows)
+        at = orthogonalize(tiles, math.sqrt(QRANK), high * (2 * QOWN), QSPAN, q_wide, q_rows)
         for half in range(2):
             for k in range(2):
-                start = pl.multiple_of(half * (QRANK // 2) + (2 * high + k) * QOWN, 8)
-                out[2 * half + k, :, :QDIM] = q_rows[pl.ds(start, QOWN), :]
+                start = pl.multiple_of(at + k * QOWN, 8)
+                out[2 * half + k, :, :QDIM] = q_rows[half, pl.ds(start, QOWN), :]
                 out[2 * half + k, :, QDIM:] = jnp.zeros((QOWN, LANES - QDIM), F32)
 
     @pl.when(z == 1)
     def _():
         tiles = [y(QMORE + t * KVDIM, QMORE + (t + 1) * KVDIM) for t in range(KVTILES)]
-        orthogonalize(tiles, math.sqrt(KVRANK), kv_rows)
+        at = orthogonalize(tiles, math.sqrt(KVRANK), high * (2 * KVOWN), KVSPAN, kv_wide, kv_rows)
         for half in range(2):
             for k in range(2):
-                start = pl.multiple_of(half * (KVRANK // 2) + (2 * high + k) * KVOWN, 8)
-                out[2 * half + k, :KVOWN, :] = kv_rows[pl.ds(start, KVOWN), :]
+                start = pl.multiple_of(at + k * KVOWN, 8)
+                out[2 * half + k, :KVOWN, :] = kv_rows[half, pl.ds(start, KVOWN), :]
                 out[2 * half + k, KVOWN:, :] = jnp.zeros((QOWN - KVOWN, LANES), F32)
 
 
@@ -240,7 +248,10 @@
     sums = lax.psum(tuple(pieces), "zh")
     leaving = jnp.concatenate(sums[: STARTS.index(QMORE)], axis=0)
     other = lax.ppermute(leaving, "zl", [(1, 0)])
-    rows = (pltpu.VMEM((QRANK, QDIM), F32), pltpu.VMEM((KVRANK, KVDIM), F32))
+    rows = [
+        pltpu.VMEM(dims, F32)
+        for dims in ((QDIM, QRANK), (KVDIM, KVRANK), (2, QSPAN, QDIM), (2, KVSPAN, KVDIM))
+    ]
     ready = call(update_kernel, shape(4, QOWN, LANES), PIECES + 1, rows)(*sums, other)
     got = lax.all_to_all(ready, ("x", "zl"), 0, 0)
     return call(join_kernel, (shape(QOWN, 2 * QDIM), shape(KVOWN, 2 * KVDIM)), 1)(got)

time: 137 us -> 136 us (level)
  no operation moved by 1% of the time
where the time goes in v6:
time: 136 us
  blocking collectives  69.3 us (51%)
  waiting for transfers between devices  29 us (21%)
  Pallas kernels  18.8 us (14%)
  starting transfers between devices  16.2 us (12%)
    psum x1, blocking collectives, body(): sums = lax.psum(tuple(pieces), 'zh')  61.4 us
    ppermute x1, waiting for transfers between devices, body(): b_got = lax.ppermute(b_send, 'zl', PAIR)  11.6 us
    pallas_call x1, Pallas kernels, body(): call(update_kernel, shape(4, QOWN, LANES), PIECES + 1, rows)(*sums, other)  9.22 us
    ppermute x1, waiting for transfers between devices, body(): other = lax.ppermute(leaving, 'zl', [(1, 0)])  8.51 us
    all_to_all x1, blocking collectives, body(): got = lax.all_to_all(ready, ('x', 'zl'), 0, 0)  7.92 us
    ppermute x1, waiting for transfers between devices, body(): b_next = lax.ppermute(b_keep[1] + b_got[1], 'x', PAIR)  5.77 us
    pallas_call x1, Pallas kernels, body(): call(send_kernel, (half, half), 4, scratch, pltpu.HBM, cost, 60)(*args)  5.72 us
    ppermute x1, starting transfers between devices, body(): b_got = lax.ppermute(b_send, 'zl', PAIR)  4.51 us
  transfers between devices with their start and end apart: 5, of which 4 were waited for; matrix products, arithmetic and copies ran while one was open for 0% of the time, Pallas kernels for 2%

profile of v6, /device:TPU:24, one launch (start us, length us, event | category | flops | bytes accessed | tf_op | source)
XLA Modules:
  0.0 135.7 jit_solution(7616355119988289806)
XLA Ops:
  0.6 0.0 copy-start.2
  0.6 0.0 copy-start.1
  0.6 0.0 copy-start
  0.7 5.7 %shard_map.60 = (f32[2,416,256]{2,1,0:T(8,128)}, f32[2,416,256]{2,1,0:T(8,128)}) custom-call(bf16[768,1536]{1,0:T(8,128)(2,1)} %ql.3, bf16[768,512]{1,0:T(8,128)(2,1)} %kl.3, bf16[768,384]{1,0:T(8,128)(2,1)} %qc.3, bf16[768,512]{1,0:T(8,128)(2,1)} %kc.3), custom_call_target="tpu_custom_call" | custom-call | flops 654311424 | bytes 8388608 | tf_op jit(solution)/shard_map/pallas_call | solution.py:240
  6.4 4.5 %collective-permute-start.2 = (f32[2,416,256]{2,1,0:T(8,128)}, f32[2,416,256]{2,1,0:T(8,128)S(1)}, u32[]{:S(2)}, u32[]{:S(2)}) collective-permute-start(f32[2,416,256]{2,1,0:T(8,128)} %get-tuple-element.75), channel_id=1, source_target_pairs={{0,16},{16,0},{1,17},{17,1},{2,18},{18,2},{3,19},{19,3},{4,20},{20... | collective-permute-start | bytes 2555912 | tf_op jit(solution)/shard_map/ppermute | solution.py:242
  10.9 3.4 %collective-permute-start = (f32[2,416,256]{2,1,0:T(8,128)}, f32[2,416,256]{2,1,0:T(8,128)S(1)}, u32[]{:S(2)}, u32[]{:S(2)}) collective-permute-start(f32[2,416,256]{2,1,0:T(8,128)} %get-tuple-element.73), channel_id=1, source_target_pairs={{0,256},{256,0},{1,257},{257,1},{2,258},{258,2},{3,259},{259,3},{4... | collective-permute-start | bytes 2555912 | tf_op jit(solution)/shard_map/ppermute | solution.py:241
  14.3 0.0 copy-done.2
  14.3 0.0 copy-done.1
  14.3 0.0 copy-done
  14.3 0.0 copy-start.3
  14.3 1.1 copy-done.3
  15.4 3.1 %shard_map.59 = (f32[2,416,256]{2,1,0:T(8,128)S(1)}, f32[2,416,256]{2,1,0:T(8,128)S(1)}) custom-call(bf16[768,1536]{1,0:T(8,128)(2,1)S(1)} %copy-done, bf16[768,512]{1,0:T(8,128)(2,1)S(1)} %copy-done.1, bf16[768,384]{1,0:T(8,128)(2,1)S(1)} %copy-done.3, bf16[768,512]{1,0:T(8,128)(2,1)S(1)} %copy-done.2), custom_call_target="tpu_custom_call" | custom-call | flops 654311424 | bytes 8388608 | tf_op jit(solution)/shard_map/pallas_call | solution.py:243
  18.5 11.6 %collective-permute-done.2.b_got = f32[2,416,256]{2,1,0:T(8,128)S(1)} collective-permute-done((f32[2,416,256]{2,1,0:T(8,128)}, f32[2,416,256]{2,1,0:T(8,128)S(1)}, u32[]{:S(2)}, u32[]{:S(2)}) %collective-permute-start.2) | collective-permute-done | bytes 852000 | tf_op jit(solution)/shard_map/ppermute | solution.py:242
  30.0 0.1 fusion
  30.1 3.4 %collective-permute-start.3 = (f32[416,256]{1,0:T(8,128)S(1)}, f32[416,256]{1,0:T(8,128)S(1)}, u32[]{:S(2)}, u32[]{:S(2)}) collective-permute-start(f32[416,256]{1,0:T(8,128)S(1)} %fusion), channel_id=1, source_target_pairs={{0,256},{256,0},{1,257},{257,1},{2,258},{258,2},{3,259},{259,3},{4... | collective-permute-start | bytes 1277960 | tf_op jit(solution)/shard_map/ppermute | solution.py:245
  33.5 0.0 collective-permute-done.a_got
  33.5 0.1 fusion.1
  33.6 3.6 %collective-permute-start.1 = (f32[416,256]{1,0:T(8,128)S(1)}, f32[416,256]{1,0:T(8,128)S(1)}, u32[]{:S(2)}, u32[]{:S(2)}) collective-permute-start(f32[416,256]{1,0:T(8,128)S(1)} %fusion.1), channel_id=1, source_target_pairs={{0,16},{16,0},{1,17},{17,1},{2,18},{18,2},{3,19},{19,3},{4,20},{20... | collective-permute-start | bytes 1277960 | tf_op jit(solution)/shard_map/ppermute | solution.py:244
  37.2 5.8 %collective-permute-done.3.b_next = f32[416,256]{1,0:T(8,128)S(1)} collective-permute-done((f32[416,256]{1,0:T(8,128)S(1)}, f32[416,256]{1,0:T(8,128)S(1)}, u32[]{:S(2)}, u32[]{:S(2)}) %collective-permute-start.3) | collective-permute-done | bytes 426016 | tf_op jit(solution)/shard_map/ppermute | solution.py:245
  43.0 3.2 %collective-permute-done.1.a_next = f32[416,256]{1,0:T(8,128)S(1)} collective-permute-done((f32[416,256]{1,0:T(8,128)S(1)}, f32[416,256]{1,0:T(8,128)S(1)}, u32[]{:S(2)}, u32[]{:S(2)}) %collective-permute-start.1) | collective-permute-done | bytes 426016 | tf_op jit(solution)/shard_map/ppermute | solution.py:244
  46.2 0.1 shard_map.61
  46.3 61.4 %all-reduce.2 = (f32[16,256]{1,0:T(8,128)S(1)}, f32[16,256]{1,0:T(8,128)S(1)}, f32[16,256]{1,0:T(8,128)S(1)}, f32[16,256]{1,0:T(8,128)S(1)}, f32[16,256]{1,0:T(8...) all-reduce(f32[16,256]{1,0:T(8,128)S(1)} %get-tuple-element.76, ...), channel_id=1, replica_groups=mesh['x'=2,'zh'=8,'zl'=2,'head'=16] {'zh'}, use_global_device_ids=true, to_apply=%region_0.0 | all-reduce | flops 212992 | bytes 1703936 | tf_op jit(solution)/shard_map/psum | solution.py:248
  108.0 1.3 collective-permute-start.4
  109.3 8.5 %collective-permute-done.4.refs_66_ = f32[320,256]{1,0:T(8,128)S(1)} collective-permute-done((f32[320,256]{1,0:T(8,128)S(1)}, f32[320,256]{1,0:T(8,128)S(1)}, u32[]{:S(2)}, u32[]{:S(2)}) %collective-permute-start.4) | collective-permute-done | bytes 327712 | tf_op jit(solution)/shard_map/ppermute | solution.py:250
  117.8 9.2 %shard_map.62 = f32[4,48,256]{2,1,0:T(8,128)S(1)} custom-call(f32[16,256]{1,0:T(8,128)S(1)} %get-tuple-element.142.refs_0_, f32[16,256]{1,0:T(8,128)S(1)} %get-tuple-element.143.refs_1_, f32[16,256]{1,0:T(8,128)S(1)} %get-tuple-element.144.refs_2_, f32[16,256]{1,0:T(8,128)S(1)} %get-tuple-element.145.refs_3_, f32[16,256]{1,0:T(8,128)S(1)} %get-tuple-element.146.refs_4_, ...), custom_call_target="tpu_custom_call" | custom-call | tf_op jit(solution)/shard_map/pallas_call | solution.py:255
  127.0 7.9 %all_to_all.5.got = f32[4,48,256]{2,1,0:T(8,128)S(1)} all-to-all(f32[4,48,256]{2,1,0:T(8,128)S(1)} %shard_map.62), channel_id=1, replica_groups=mesh['x'=2,'zh'=8,'zl'=2,'head'=16] {'x','zl'}, dimensions={0} | all-to-all | bytes 393216 | tf_op jit(solution)/shard_map/all_to_all | solution.py:256
  134.9 0.7 shard_map.63
  (20 shorter events, 0.1 us)
Async XLA Ops:
  0.6 13.7 %copy-start.2 = (bf16[768,512]{1,0:T(8,128)(2,1)S(1)}, bf16[768,512]{1,0:T(8,128)(2,1)}, u32[]{:S(2)}) copy-start(bf16[768,512]{1,0:T(8,128)(2,1)} %kc.3) | copy-start | bytes 2359300
  0.6 13.7 %copy-start.1 = (bf16[768,512]{1,0:T(8,128)(2,1)S(1)}, bf16[768,512]{1,0:T(8,128)(2,1)}, u32[]{:S(2)}) copy-start(bf16[768,512]{1,0:T(8,128)(2,1)} %kl.3) | copy-start | bytes 2359300
  0.6 13.7 %copy-start = (bf16[768,1536]{1,0:T(8,128)(2,1)S(1)}, bf16[768,1536]{1,0:T(8,128)(2,1)}, u32[]{:S(2)}) copy-start(bf16[768,1536]{1,0:T(8,128)(2,1)} %ql.3) | copy-start | bytes 7077892
  6.4 23.7 %collective-permute-start.2 = (f32[2,416,256]{2,1,0:T(8,128)}, f32[2,416,256]{2,1,0:T(8,128)S(1)}, u32[]{:S(2)}, u32[]{:S(2)}) collective-permute-start(f32[2,416,256]{2,1,0:T(8,128)} %get-tuple-element.75), channel_id=1, source_target_pairs={{0,16},{16,0},{1,17},{17,1},{2,18},{18,2},{3,19},{19,3},{4,20},{20... | collective-permute-start | bytes 2555912 | tf_op jit(solution)/shard_map/ppermute | solution.py:242
  10.9 22.6 %collective-permute-start = (f32[2,416,256]{2,1,0:T(8,128)}, f32[2,416,256]{2,1,0:T(8,128)S(1)}, u32[]{:S(2)}, u32[]{:S(2)}) collective-permute-start(f32[2,416,256]{2,1,0:T(8,128)} %get-tuple-element.73), channel_id=1, source_target_pairs={{0,256},{256,0},{1,257},{257,1},{2,258},{258,2},{3,259},{259,3},{4... | collective-permute-start | bytes 2555912 | tf_op jit(solution)/shard_map/ppermute | solution.py:241
  14.3 1.1 copy-start.3
  30.1 12.9 %collective-permute-start.3 = (f32[416,256]{1,0:T(8,128)S(1)}, f32[416,256]{1,0:T(8,128)S(1)}, u32[]{:S(2)}, u32[]{:S(2)}) collective-permute-start(f32[416,256]{1,0:T(8,128)S(1)} %fusion), channel_id=1, source_target_pairs={{0,256},{256,0},{1,257},{257,1},{2,258},{258,2},{3,259},{259,3},{4... | collective-permute-start | bytes 1277960 | tf_op jit(solution)/shard_map/ppermute | solution.py:245
  33.6 12.6 %collective-permute-start.1 = (f32[416,256]{1,0:T(8,128)S(1)}, f32[416,256]{1,0:T(8,128)S(1)}, u32[]{:S(2)}, u32[]{:S(2)}) collective-permute-start(f32[416,256]{1,0:T(8,128)S(1)} %fusion.1), channel_id=1, source_target_pairs={{0,16},{16,0},{1,17},{17,1},{2,18},{18,2},{3,19},{19,3},{4,20},{20... | collective-permute-start | bytes 1277960 | tf_op jit(solution)/shard_map/ppermute | solution.py:244
  108.0 9.8 %collective-permute-start.4 = (f32[320,256]{1,0:T(8,128)S(1)}, f32[320,256]{1,0:T(8,128)S(1)}, u32[]{:S(2)}, u32[]{:S(2)}) collective-permute-start(f32[320,256]{1,0:T(8,128)S(1)} %constant_dynamic-update-slice_fusion), channel_id=1, source_target_pairs={{16,0},{17,1},{18,2},{19,3},{20,4},{21,5},{22,6},{23,7},{24,8},{25... | collective-permute-start | bytes 983048 | tf_op jit(solution)/shard_map/ppermute | solution.py:250
